TPU v7x, 256 devices: a whole 4x4x8 slice. The times are simulated.
256 devices in a mesh: enc: 8 (over z), seq: 16 (over y, x), mp: 2 (over core).
Axes of the slice: x: 4, y: 4, z: 8, core: 2. Of those that a mesh axis runs over, the one named last changes fastest.
Arguments:
- images: bfloat16 [2048, 64, 1280], P(('enc', 'seq', 'mp')), may hold values from -6 to 6
- vit_gain: float32 [1280], replicated, may hold values from 0.5 to 3
- vit_qkv: bfloat16 [1280, 1920], P(('enc', 'mp')), may hold values from -0.15625 to 0.15625
- vit_out: bfloat16 [640, 1280], P(('enc', 'mp')), may hold values from -0.25 to 0.25
- kv_weight: bfloat16 [1280, 1024], P('mp'), may hold values from -0.15625 to 0.15625
- queries: bfloat16 [32768, 4096], P(('enc', 'seq', 'mp')), may hold values from -6 to 6
- q_gain: float32 [128], replicated, may hold values from 0.6 to 3
- k_gain: float32 [128], replicated, may hold values from 0.6 to 3
- out_grad: bfloat16 [32768, 4096], P(('enc', 'seq', 'mp')), may hold values from -6 to 6
- block_image: int32 [2048], P(('enc', 'seq', 'mp')), may hold values from 0 to 7, as said below
- block_dest: int32 [2048], P(('enc', 'seq', 'mp')), may hold values from 0 to 255, as said below
- key_image: int32 [1024, 4], P(('enc', 'seq', 'mp')), may hold values from 0 to 4, as said below
- text_seen: int32 [32768], P(('enc', 'seq', 'mp')), may hold values from 1 to 4, as said below
Outputs:
- attended: bfloat16 [32768, 4096], P(('enc', 'seq', 'mp'))
- kv_grad: bfloat16 [2048, 64, 1024], P(('enc', 'seq', 'mp'))
Inputs may be any that keep to these rules, and one draw needn't show every extreme that they name: `block_image`: on each device blocks are numbered by image from 0, rising by one at each new image; an image is one block or the two blocks 2j and 2j+1 of its device. `block_dest`: blocks 2j and 2j+1 of a device go to one device of its seq group; the pairs of a device are spread evenly over the group, so no device sends more than 2 blocks to another and some device sends exactly 2 to some other; every device receives exactly 8 blocks. Every key block receives at most one block; a sequence's blocks fill its first key blocks, 1 to 4 of them, and some sequence holds 4. The blocks of one image go to one sequence, in consecutive key blocks. `key_image`: the image number of a key block within its sequence, counted from 0 in key-block order, or 4 where the key block is empty; it agrees with block_dest and block_image. A text token sees the first text_seen images of its sequence: at least 1, at most the sequence's number of images.
All inputs are finite; a program needn't handle non-finite values.
Results may differ from a plain program's by a relative error of at most 0.034.
The roundings to bfloat16 on the way count: a program that leaves them out, or rounds other values in their place, can miss the bound.
Values may be sent and summed in bfloat16 or wider, within the bound.
A program may use at most 64 MiB of HBM per device.

v0:
```python
import functools
import math

import jax
import jax.numpy as jnp
from jax import lax
from jax.experimental import pallas as pl
from jax.experimental.pallas import tpu as pltpu
from jax.sharding import PartitionSpec as P

VHEADS = 8
VHEAD = 80
HEAD = 128
KVHEADS = 4
SHARED = 8
BLK = 64
LEN = 32
CAP = 4
PEERS = 16
PAIRS = 4
PIECES = 2
PER = KVHEADS // PIECES
WIDE = PER * 2 * HEAD
EPS = 1e-05
MESH = pl.DeviceIdType.MESH
f32 = jnp.float32
bf16 = jnp.bfloat16


def dot_nn(left, right):
    return jnp.dot(left, right, preferred_element_type=f32)


def dot_nt(left, right):
    return lax.dot_general(left, right, (((1,), (1,)), ((), ())), preferred_element_type=f32)


def dot_tn(left, right):
    return lax.dot_general(left, right, (((0,), (0,)), ((), ())), preferred_element_type=f32)


def greet(axis, count, me):
    barrier = pltpu.get_barrier_semaphore()

    def body(step, carry):
        peer = lax.rem(me + step, count)
        pl.semaphore_signal(barrier, inc=1, device_id={axis: peer}, device_id_type=MESH)
        return carry

    lax.fori_loop(1, count, body, 0)
    pl.semaphore_wait(barrier, count - 1)


def exchange(source, target, me, send_sem, recv_sem):
    def body(step, carry):
        peer = lax.rem(me + step, PEERS)
        pltpu.make_async_remote_copy(
            src_ref=source.at[peer],
            dst_ref=target.at[me],
            send_sem=send_sem,
            recv_sem=recv_sem,
            device_id={"seq": peer},
            device_id_type=MESH,
        ).start()
        return carry

    lax.fori_loop(1, PEERS, body, 0)
    target[me] = source[me]


def wait_all(buffer, sem):
    view = buffer.at[pl.ds(0, PEERS - 1)]
    pltpu.make_async_copy(view, view, sem).wait()


def reach_all(step_map, doublings):
    total = None
    power = step_map
    for index in range(doublings):
        if total is None:
            n = step_map.shape[0]
            eye = lax.broadcasted_iota(jnp.int32, (n, n), 0) == lax.broadcasted_iota(
                jnp.int32, (n, n), 1
            )
            total = jnp.where(eye, 1.0, 0.0) + power
        else:
            total = total + dot_nn(total.astype(bf16), power.astype(bf16))
        if index < doublings - 1:
            power = dot_nn(power.astype(bf16), power.astype(bf16))
    return total


def split_colors(src_partner, dst_partner, doublings):
    n = src_partner.shape[0]
    row = lax.broadcasted_iota(jnp.int32, (n, n), 0)
    col = lax.broadcasted_iota(jnp.int32, (n, n), 1)
    src_f = jnp.where(src_partner, 1.0, 0.0)
    dst_f = jnp.where(dst_partner, 1.0, 0.0)
    orbit = reach_all(dot_nn(src_f.astype(bf16), dst_f.astype(bf16)), doublings) > 0.5
    lead_c = jnp.min(jnp.where(orbit, col, n), axis=1, keepdims=True)
    lead_r = jnp.min(jnp.where(orbit, row, n), axis=0, keepdims=True)
    other_c = jnp.sum(jnp.where(src_partner, lead_r, 0), axis=1, keepdims=True)
    other_r = jnp.sum(jnp.where(src_partner, lead_c, 0), axis=0, keepdims=True)
    return (lead_c < other_c).astype(jnp.int32), (lead_r < other_r).astype(jnp.int32)


def color_tables(dest, me):
    n = dest.shape[0]
    row = lax.broadcasted_iota(jnp.int32, (n, n), 0)
    col = lax.broadcasted_iota(jnp.int32, (n, n), 1)
    dest_t = jnp.transpose(dest.astype(f32)).astype(jnp.int32)
    owner_c, owner_r = dest >> 4, dest_t >> 4
    parity_same = (row & 1) == (col & 1)
    src_same = ((row >> 3) == (col >> 3)) & parity_same
    dst_same = (owner_c == owner_r) & parity_same
    rank_c = jnp.sum(jnp.where(dst_same & (col < row), 1, 0), axis=1, keepdims=True)
    rank_r = jnp.sum(jnp.where(dst_same & (row < col), 1, 0), axis=0, keepdims=True)
    src_partner = col == (row ^ 2)
    dst_partner = dst_same & (rank_r == (rank_c ^ 1))
    one_c, one_r = split_colors(src_partner, dst_partner, 5)
    alike = (one_c == one_r) & (row != col)
    two_c, _ = split_colors(src_same & alike, dst_same & alike, 4)
    color = jnp.broadcast_to(2 * one_c + two_c, (n, n))
    src = row >> 3
    pair = (row & 7) >> 1
    half = row & 1
    even = half == 0
    mine = src == me
    turn = me >> 2

    def pick(mask, value):
        return jnp.sum(jnp.where(mask, value, 0), axis=0, keepdims=True)

    rows = [
        pick(mine & even & (color == col), pair),
        pick(mine & even & (pair == col), color),
        pick(even & (color == turn) & (owner_c == col), src),
        pick(even & (color == turn) & (src == col), owner_c),
        pick((owner_c == me) & ((dest & 15) == col), 2 * color + half + 1) - 1,
        pick((owner_c == me) & (2 * color + half == col), dest & 15),
    ]
    rows += [jnp.zeros_like(rows[0])] * 2
    return jnp.concatenate(rows, axis=0)


def tables_kernel(dest_ref, tab_ref, every, send_sem, recv_sem):
    me = lax.axis_index("seq")
    greet("seq", PEERS, me)

    def body(step, carry):
        peer = lax.rem(me + step, PEERS)
        pltpu.make_async_remote_copy(
            src_ref=dest_ref,
            dst_ref=every.at[me],
            send_sem=send_sem,
            recv_sem=recv_sem,
            device_id={"seq": peer},
            device_id_type=MESH,
        ).start()
        return carry

    lax.fori_loop(1, PEERS, body, 0)
    every[me] = dest_ref[...]
    wait_all(every, recv_sem)
    wait_all(every, send_sem)
    tab_ref[...] = color_tables(every[...].reshape(PEERS * 8, 128), me)


def encoder_kernel(
    tab_ref, image_ref, x_ref, gain_ref, qkv_ref, out_ref, kv_ref, pay_ref, normed, mixed, att, hidden
):
    tokens, vis = x_ref.shape
    span = 2 * BLK

    def norm_rows(t, carry):
        rows = pl.ds(pl.multiple_of(t * 64, 64), 64)
        values = x_ref[rows, :].astype(f32)
        center = values - jnp.mean(values, axis=-1, keepdims=True)
        spread = jnp.mean(center * center, axis=-1, keepdims=True)
        normed[rows, :] = (center * lax.rsqrt(spread + EPS) * gain_ref[...]).astype(bf16)
        return carry

    lax.fori_loop(0, tokens // 64, norm_rows, 0)

    def mix_columns(t, carry):
        cols = pl.ds(pl.multiple_of(t * 384, 128), 384)
        mixed[:, cols] = dot_nn(normed[...], qkv_ref[:, cols]).astype(bf16)
        return carry

    lax.fori_loop(0, mixed.shape[1] // 384, mix_columns, 0)

    width = VHEADS * VHEAD
    scale = 1.0 / math.sqrt(VHEAD)
    row = lax.broadcasted_iota(jnp.int32, (span, span), 0)
    col = lax.broadcasted_iota(jnp.int32, (span, span), 1)
    near = (row // BLK) == (col // BLK)

    def attend(j, carry):
        rows = pl.ds(pl.multiple_of(j * span, span), span)
        joined = image_ref[2 * j] == image_ref[2 * j + 1]
        allowed = near | joined
        tiles = [None] * (width // 128)
        for head in range(VHEADS):
            first, last = head * VHEAD // 128, ((head + 1) * VHEAD - 1) // 128
            cut = (last - first + 1) * 128
            base = first * 128
            lane = lax.broadcasted_iota(jnp.int32, (span, cut), 1) + base
            inside = (lane >= head * VHEAD) & (lane < (head + 1) * VHEAD)
            q = jnp.where(inside, mixed[rows, base : base + cut], jnp.zeros((), bf16))
            k = mixed[rows, width + base : width + base + cut]
            v = mixed[rows, 2 * width + base : 2 * width + base + cut]
            scores = jnp.where(allowed, dot_nt(k, q) * scale, -jnp.inf)
            terms = jnp.exp(scores - jnp.max(scores, axis=0, keepdims=True))
            weights = (terms / jnp.sum(terms, axis=0, keepdims=True)).astype(bf16)
            result = dot_tn(weights, v)
            for tile in range(first, last + 1):
                at = (tile - first) * 128
                part = result[:, at : at + 128]
                if tiles[tile] is None:
                    tiles[tile] = part
                else:
                    tiles[tile] = jnp.where(inside[:, at : at + 128], part, tiles[tile])
        att[rows, :] = jnp.concatenate(tiles, axis=1).astype(bf16)
        return carry

    lax.fori_loop(0, tokens // span, attend, 0)

    def project(t, carry):
        cols = pl.ds(pl.multiple_of(t * 256, 256), 256)
        part = x_ref[:, cols].astype(f32) + dot_nn(att[...], out_ref[:, cols])
        hidden[:, :, cols] = part.astype(bf16).reshape(PAIRS, span, 256)
        return carry

    lax.fori_loop(0, vis // 256, project, 0)

    half = KVHEADS * HEAD
    for piece in range(PIECES):

        def make_pay(t, carry):
            source = jnp.concatenate([hidden[tab_ref[0, c]] for c in range(PAIRS)], axis=0)
            at = pl.multiple_of((piece * PER + t) * HEAD, HEAD)
            weight = jnp.concatenate(
                [kv_ref[:, pl.ds(at, HEAD)], kv_ref[:, pl.ds(half + at, HEAD)]], axis=1
            )
            got = dot_nn(source, weight).astype(bf16).reshape(PEERS, span // 4, 2 * HEAD)
            pay_ref[piece, :, :, pl.ds(pl.multiple_of(t * 2 * HEAD, 2 * HEAD), 2 * HEAD)] = got
            return carry

        lax.fori_loop(0, PER, make_pay, 0)


def cross_kernel(
    tab_ref,
    kimg_ref,
    seen_ref,
    pay_ref,
    q_ref,
    og_ref,
    qg_ref,
    kg_ref,
    att_ref,
    kvg_ref,
    qn,
    got1,
    out2,
    got2,
    gkv,
    out3,
    got3,
    out4,
    got4,
    send_sem,
    recv_sem,
):
    me = lax.axis_index("seq")
    scale = 1.0 / math.sqrt(HEAD)
    greet("seq", PEERS, me)
    for h in range(PIECES):
        exchange(pay_ref.at[h], got1[h], me, send_sem.at[0, h], recv_sem.at[0, h])

    def norm_queries(g, carry):
        block = q_ref[:, pl.ds(pl.multiple_of(g * SHARED * HEAD, HEAD), SHARED * HEAD)]
        for hh in range(SHARED):
            x = block[:, hh * HEAD : (hh + 1) * HEAD].astype(f32)
            inv = lax.rsqrt(jnp.mean(x * x, axis=-1, keepdims=True) + EPS)
            y = (x * inv * qg_ref[...]).astype(bf16)
            for s in range(CAP):
                qn[g, s, hh * LEN : (hh + 1) * LEN, :] = y[s * LEN : (s + 1) * LEN, :]
        return carry

    lax.fori_loop(0, KVHEADS, norm_queries, 0)

    def relay(h, got, out, row, target, phase):
        wait_all(got[h], recv_sem.at[phase - 1, h])

        def body(d, carry):
            out[h][d] = got[h][tab_ref[row, d]]
            return carry

        lax.fori_loop(0, PEERS, body, 0)
        exchange(out[h], target[h], me, send_sem.at[phase, h], recv_sem.at[phase, h])

    def one(h, gi, s):
        g = h * PER + gi
        at = pl.multiple_of(gi * 2 * HEAD, 2 * HEAD)
        blocks, masks = [], []
        seen = seen_ref[pl.ds(s, 1), :]
        for kb in range(CAP):
            index = tab_ref[4, s * CAP + kb]
            block = got2[h][pl.ds(2 * jnp.maximum(index, 0), 2), :, pl.ds(at, 2 * HEAD)]
            blocks.append(
                jnp.where(index >= 0, block, jnp.zeros((), bf16)).reshape(BLK, 2 * HEAD)
            )
            visible = kimg_ref[s, kb] < seen
            masks.append(jnp.broadcast_to(visible, (BLK, SHARED * LEN)))
        keyval = jnp.concatenate(blocks, axis=0)
        allowed = jnp.concatenate(masks, axis=0)
        keys = keyval[:, :HEAD].astype(f32)
        values = keyval[:, HEAD:]
        inv = lax.rsqrt(jnp.mean(keys * keys, axis=-1, keepdims=True) + EPS)
        kn = (keys * inv * kg_ref[...]).astype(bf16)
        queries = qn[g, s]
        rows = pl.ds(pl.multiple_of(s * LEN, LEN), LEN)
        col0 = pl.multiple_of(g * SHARED * HEAD, SHARED * HEAD)
        grad_row = og_ref[rows, pl.ds(col0, SHARED * HEAD)]
        grads = jnp.concatenate(
            [grad_row[:, hh * HEAD : (hh + 1) * HEAD] for hh in range(SHARED)], axis=0
        )
        scores = jnp.where(allowed, dot_nt(kn, queries) * scale, -jnp.inf)
        terms = jnp.exp(scores - jnp.max(scores, axis=0, keepdims=True))
        weights = terms / jnp.sum(terms, axis=0, keepdims=True)
        rounded = weights.astype(bf16)
        attended = dot_tn(rounded, values).astype(bf16)
        att_ref[rows, pl.ds(col0, SHARED * HEAD)] = jnp.concatenate(
            [attended[hh * LEN : (hh + 1) * LEN, :] for hh in range(SHARED)], axis=1
        )
        grad_values = dot_nn(rounded, grads)
        grad_dot = dot_nt(values, grads)
        delta = jnp.sum(weights * grad_dot, axis=0, keepdims=True)
        grad_scores = (weights * (grad_dot - delta) * scale).astype(bf16)
        gained = dot_nn(grad_scores, queries) * kg_ref[...]
        mean = jnp.mean(keys * gained, axis=-1, keepdims=True)
        grad_keys = inv * (gained - keys * inv * inv * mean)
        result = jnp.concatenate([grad_keys, grad_values], axis=1).astype(bf16)
        gkv[pl.ds(s * CAP, CAP), :, pl.ds(at, 2 * HEAD)] = result.reshape(CAP, BLK, 2 * HEAD)

    def attend(h):
        wait_all(got2[h], recv_sem.at[1, h])

        def body(step, carry):
            gi, s = step // (CAP // 2), lax.rem(step, CAP // 2) * 2
            one(h, gi, s)
            one(h, gi, s + 1)
            return carry

        lax.fori_loop(0, PER * CAP // 2, body, 0)

        def pack(cb, carry):
            block = gkv[tab_ref[5, cb]]
            out3[h][pl.ds(2 * cb, 2)] = block.reshape(2, BLK // 2, WIDE)
            return carry

        lax.fori_loop(0, 2 * PAIRS, pack, 0)
        exchange(out3[h], got3[h], me, send_sem.at[2, h], recv_sem.at[2, h])

    for h in range(PIECES):
        relay(h, got1, out2, 2, got2, 1)
    for h in range(PIECES):
        attend(h)
        if h > 0:
            relay(h - 1, got3, out4, 3, got4, 3)
    relay(PIECES - 1, got3, out4, 3, got4, 3)
    half = KVHEADS * HEAD
    for h in range(PIECES):
        wait_all(got4[h], recv_sem.at[3, h])
        for j in range(PAIRS):
            color = tab_ref[1, j]
            block = got4[h][pl.ds(4 * color, 4)].reshape(2, BLK, WIDE)
            for gi in range(PER):
                at = (h * PER + gi) * HEAD
                kvg_ref[2 * j : 2 * j + 2, :, at : at + HEAD] = block[
                    :, :, gi * 2 * HEAD : gi * 2 * HEAD + HEAD
                ]
                kvg_ref[2 * j : 2 * j + 2, :, half + at : half + at + HEAD] = block[
                    :, :, gi * 2 * HEAD + HEAD : (gi + 1) * 2 * HEAD
                ]
    for phase in range(4):
        for h in range(PIECES):
            wait_all(got1[h], send_sem.at[phase, h])


VMEM = pl.BlockSpec(memory_space=pltpu.VMEM)
SMEM = pl.BlockSpec(memory_space=pltpu.SMEM)
LIMIT = 48 * 1024 * 1024


def local(
    images,
    vit_gain,
    vit_qkv,
    vit_out,
    kv_weight,
    queries,
    q_gain,
    k_gain,
    out_grad,
    block_image,
    block_dest,
    key_image,
    text_seen,
):
    enc_blocks, block_len, vis = images.shape
    tokens = enc_blocks * block_len
    full_qkv = lax.all_gather(vit_qkv, ("enc", "mp"), axis=0, tiled=True)
    full_out = lax.all_gather(vit_out, ("enc", "mp"), axis=0, tiled=True)
    full_kv = lax.all_gather(kv_weight, "mp", axis=0, tiled=True)
    tables = pl.pallas_call(
        tables_kernel,
        out_shape=jax.ShapeDtypeStruct((8, 128), jnp.int32),
        in_specs=[VMEM],
        out_specs=VMEM,
        scratch_shapes=[
            pltpu.VMEM((PEERS, 8, 128), jnp.int32),
            pltpu.SemaphoreType.DMA,
            pltpu.SemaphoreType.DMA,
        ],
        compiler_params=pltpu.CompilerParams(collective_id=0, has_side_effects=True),
    )(jnp.broadcast_to(block_dest[:, None], (8, 128)))
    slots = (PIECES, PEERS, BLK // 2, WIDE)
    payload = pl.pallas_call(
        encoder_kernel,
        out_shape=jax.ShapeDtypeStruct(slots, bf16),
        in_specs=[SMEM, SMEM] + [VMEM] * 5,
        out_specs=VMEM,
        scratch_shapes=[
            pltpu.VMEM((tokens, vis), bf16),
            pltpu.VMEM((tokens, 3 * VHEADS * VHEAD), bf16),
            pltpu.VMEM((tokens, VHEADS * VHEAD), bf16),
            pltpu.VMEM((PAIRS, 2 * BLK, vis), bf16),
        ],
        compiler_params=pltpu.CompilerParams(vmem_limit_bytes=LIMIT),
    )(
        tables,
        block_image,
        images.reshape(tokens, vis),
        vit_gain.reshape(1, vis),
        full_qkv,
        full_out,
        full_kv,
    )
    seen = jnp.tile(text_seen.reshape(CAP, 1, LEN), (1, SHARED, 1)).reshape(CAP, SHARED * LEN)
    attended, kv_grad = pl.pallas_call(
        cross_kernel,
        out_shape=(
            jax.ShapeDtypeStruct(queries.shape, bf16),
            jax.ShapeDtypeStruct((enc_blocks, block_len, 2 * KVHEADS * HEAD), bf16),
        ),
        in_specs=[SMEM, SMEM] + [VMEM] * 6,
        out_specs=(VMEM, VMEM),
        scratch_shapes=[pltpu.VMEM((KVHEADS, CAP, SHARED * LEN, HEAD), bf16)]
        + [[pltpu.VMEM(slots[1:], bf16)] * PIECES] * 3
        + [pltpu.VMEM((CAP * CAP, BLK, WIDE), bf16)]
        + [[pltpu.VMEM(slots[1:], bf16)] * PIECES] * 4
        + [pltpu.SemaphoreType.DMA((4, PIECES))] * 2,
        compiler_params=pltpu.CompilerParams(
            collective_id=1, has_side_effects=True, vmem_limit_bytes=LIMIT
        ),
    )(
        tables,
        key_image,
        seen,
        payload,
        queries,
        out_grad,
        q_gain.reshape(1, HEAD),
        k_gain.reshape(1, HEAD),
    )
    return attended, kv_grad


def solution(mesh):
    everywhere = ("enc", "seq", "mp")
    placed = (
        P(everywhere, None, None),
        P(),
        P(("enc", "mp"), None),
        P(("enc", "mp"), None),
        P("mp", None),
        P(everywhere, None),
        P(),
        P(),
        P(everywhere, None),
        P(everywhere),
        P(everywhere),
        P(everywhere, None),
        P(everywhere),
    )
    return jax.shard_map(
        local,
        mesh=mesh,
        in_specs=placed,
        out_specs=(P(everywhere, None), P(everywhere, None, None)),
        check_vma=False,
    )
```

profile of v0, /device:TPU:32, one launch (start us, length us, event | category | flops | bytes accessed | tf_op | source)
XLA Modules:
  0.0 205.5 jit_solution(7589251718877885655)
XLA Ops:
  7.2 0.0 copy-start.10
  7.2 0.0 copy-start.9
  7.2 0.0 copy-start.11
  7.2 0.0 copy-start.1
  7.2 0.0 copy-start.6
  7.2 0.0 all-gather.8.cloned.1.call-start
  7.3 0.7 all-gather.8.cloned.1.call-update
  7.9 0.0 all-gather.6.cloned.1.call-start
  8.0 0.7 all-gather.6.cloned.1.call-update
  8.7 0.0 all-gather.4.cloned.1.call-start
  8.7 0.7 all-gather.4.cloned.1.call-update
  9.4 0.0 copy-done.10
  9.4 0.7 broadcast_in_dim.2.dest_ref
  10.1 12.7 %shard_map.140.tab_ref = s32[8,128]{1,0:T(8,128)} custom-call(s32[8,128]{1,0:T(8,128)} %broadcast_in_dim.2.dest_ref), custom_call_target="tpu_custom_call" | custom-call | tf_op jit(solution)/shard_map/pallas_call | solution.py:417
  22.9 0.0 copy-done.9
  22.9 0.0 copy-done.11
  22.9 0.1 tile.9
  23.0 0.1 tile.11.seen_ref
  23.1 6.1 %all-gather.8.cloned.1.call-done.kv_ref = bf16[1280,1024]{1,0:T(8,128)(2,1)} async-done(((bf16[640,1024]{1,0:T(8,128)(2,1)}), bf16[1280,1024]{1,0:T(8,128)(2,1)}) %all-gather.8.cloned.1.call-update) | async-done | bytes 2621456 | tf_op jit(solution)/shard_map/all_gather | solution.py:416
  29.2 41.9 %all-gather.6.cloned.1.call-done.out_ref = bf16[640,1280]{1,0:T(8,128)(2,1)} async-done(((bf16[40,1280]{1,0:T(8,128)(2,1)}), bf16[640,1280]{1,0:T(8,128)(2,1)}) %all-gather.6.cloned.1.call-update) | async-done | bytes 1638416 | tf_op jit(solution)/shard_map/all_gather | solution.py:415
  71.1 43.7 %all-gather.4.cloned.1.call-done.qkv_ref = bf16[1280,1920]{1,0:T(8,128)(2,1)} async-done(((bf16[80,1920]{1,0:T(8,128)(2,1)}), bf16[1280,1920]{1,0:T(8,128)(2,1)}) %all-gather.4.cloned.1.call-update) | async-done | bytes 4915216 | tf_op jit(solution)/shard_map/all_gather | solution.py:414
  114.8 0.0 copy-done.1
  114.8 0.0 copy-done.6
  114.8 0.0 copy-start
  114.8 1.4 copy-done
  116.2 0.0 copy-start.4
  116.2 0.7 copy-done.4
  116.9 0.0 copy-start.2
  116.9 0.0 copy-start.3
  116.9 0.0 copy-start.5
  116.9 0.0 copy-start.7
  116.9 0.0 copy-start.8
  116.9 20.1 %shard_map.141.pay_ref = bf16[2,16,32,512]{3,2,1,0:T(8,128)(2,1)S(1)} custom-call(s32[8,128]{1,0:T(8,128)S(1)} %copy-done.4, s32[8]{0:T(128)S(1)} %copy-done.6, bf16[512,1280]{1,0:T(8,128)(2,1)S(1)} %bitcast.7, f32[1,1280]{1,0:T(1,128)S(1)} %reshape.22.gain_ref, bf16[1280,1920]{1,0:T(8,128)(2,1)} %all-gather.4.cloned.1.call-done.qkv_ref, ...), custom_call_target="tpu_custom_call" | custom-call | tf_op jit(solution)/shard_map/pallas_call | solution.py:430
  137.0 0.0 copy-done.2
  137.0 0.0 copy-done.3
  137.0 0.0 copy-done.5
  137.1 0.0 copy-done.7
  137.1 0.0 copy-done.8
  137.1 59.9 %shard_map.142 = (bf16[128,4096]{1,0:T(8,128)(2,1)S(1)}, bf16[8,64,1024]{2,1,0:T(8,128)(2,1)S(1)}) custom-call(s32[8,128]{1,0:T(8,128)S(1)} %copy-done.4, s32[4,4]{1,0:T(4,128)S(1)} %copy-done.5, s32[4,256]{1,0:T(4,128)S(1)} %tile.11.seen_ref, bf16[2,16,32,512]{3,2,1,0:T(8,128)(2,1)S(1)} %shard_map.141.pay_ref, bf16[128,4096]{1,0:T(8,128)(2,1)S(1)} %copy-done.2, ...), custom_call_target="tpu_custom_call" | custom-call | tf_op jit(solution)/shard_map/pallas_call | solution.py:452
  197.0 1.0 copy.17
  198.0 1.0 copy.18
  (2 shorter events, 0.0 us)
Async XLA Ops:
  7.2 2.3 %copy-start.10 = (s32[8]{0:T(128)S(1)}, s32[8]{0:T(128)}, u32[]{:S(2)}) copy-start(s32[8]{0:T(128)} %param.23) | copy-start | bytes 100
  7.2 15.7 %copy-start.9 = (f32[1280]{0:T(1024)S(1)}, f32[1280]{0:T(1024)}, u32[]{:S(2)}) copy-start(f32[1280]{0:T(1024)} %param.14) | copy-start | bytes 15364
  7.2 15.7 %copy-start.11 = (s32[128]{0:T(128)S(1)}, s32[128]{0:T(128)}, u32[]{:S(2)}) copy-start(s32[128]{0:T(128)} %param.25) | copy-start | bytes 1540
  7.2 107.6 %copy-start.1 = (bf16[8,64,1280]{2,1,0:T(8,128)(2,1)S(1)}, bf16[8,64,1280]{2,1,0:T(8,128)(2,1)}, u32[]{:S(2)}) copy-start(bf16[8,64,1280]{2,1,0:T(8,128)(2,1)} %param.13) | copy-start | bytes 3932164
  7.2 107.6 %copy-start.6 = (s32[8]{0:T(128)S(1)}, s32[8]{0:T(128)}, u32[]{:S(2)}) copy-start(s32[8]{0:T(128)} %image_ref.1) | copy-start | bytes 100
  7.2 22.0 %all-gather.8.cloned.1.call-start = ((), (), s32[]{:S(2)}) async-start(), calls=%async_computation.2 | async-start | bytes 3932160 | tf_op jit(solution)/shard_map/all_gather | solution.py:416
  7.9 63.1 %all-gather.6.cloned.1.call-start = ((), (), s32[]{:S(2)}) async-start(), calls=%async_computation.1 | async-start | bytes 1740800 | tf_op jit(solution)/shard_map/all_gather | solution.py:415
  8.7 106.1 %all-gather.4.cloned.1.call-start = ((), (), s32[]{:S(2)}) async-start(), calls=%async_computation | async-start | bytes 5222400 | tf_op jit(solution)/shard_map/all_gather | solution.py:414
  114.8 1.4 copy-start
  116.2 0.7 copy-start.4
  116.9 20.1 %copy-start.2 = (bf16[128,4096]{1,0:T(8,128)(2,1)S(1)}, bf16[128,4096]{1,0:T(8,128)(2,1)}, u32[]{:S(2)}) copy-start(bf16[128,4096]{1,0:T(8,128)(2,1)} %q_ref.1) | copy-start | bytes 3145732
  116.9 20.1 %copy-start.3 = (bf16[128,4096]{1,0:T(8,128)(2,1)S(1)}, bf16[128,4096]{1,0:T(8,128)(2,1)}, u32[]{:S(2)}) copy-start(bf16[128,4096]{1,0:T(8,128)(2,1)} %og_ref.1) | copy-start | bytes 3145732
  116.9 20.1 %copy-start.5 = (s32[4,4]{1,0:T(4,128)S(1)}, s32[4,4]{1,0:T(4,128)}, u32[]{:S(2)}) copy-start(s32[4,4]{1,0:T(4,128)} %kimg_ref.1) | copy-start | bytes 196
  116.9 20.2 %copy-start.7 = (f32[128]{0:T(128)S(1)}, f32[128]{0:T(128)}, u32[]{:S(2)}) copy-start(f32[128]{0:T(128)} %param.19) | copy-start | bytes 1540
  116.9 20.2 %copy-start.8 = (f32[128]{0:T(128)S(1)}, f32[128]{0:T(128)}, u32[]{:S(2)}) copy-start(f32[128]{0:T(128)} %param.20) | copy-start | bytes 1540
Sparse Core Ops, SparseCore 0:
  9.8 19.2 all-gather.7
  31.0 40.0 all-gather.5
  72.9 41.8 all-gather.3
where the time goes:
time: 206 us
  waiting for transfers between devices  93.8 us (46%)
  Pallas kernels  92.8 us (45%)
  between operations  13.9 us (7%)
  local copies, waits for them, and re-layouts  4.93 us (2%)
    pallas_call x1, Pallas kernels, local(): pl.pallas_call(cross_kernel, out_shape=(jax.ShapeDtypeStruct(queries.shap...  59.9 us
    all_gather x1, waiting for transfers between devices, local(): full_qkv = lax.all_gather(vit_qkv, ('enc', 'mp'), axis=0, tiled=True)  43.7 us
    all_gather x1, waiting for transfers between devices, local(): full_out = lax.all_gather(vit_out, ('enc', 'mp'), axis=0, tiled=True)  41.9 us
    pallas_call x1, Pallas kernels, local(): pl.pallas_call(encoder_kernel, out_shape=jax.ShapeDtypeStruct(slots, bf16...  20.1 us
    pallas_call x1, Pallas kernels, local(): pl.pallas_call(tables_kernel, out_shape=jax.ShapeDtypeStruct((8, 128), jn...  12.7 us
    all_gather x1, waiting for transfers between devices, local(): full_kv = lax.all_gather(kv_weight, 'mp', axis=0, tiled=True)  6.12 us
  transfers between devices with their start and end apart: 3, of which 3 were waited for; matrix products, arithmetic and copies ran while one was open for 0% of the time, Pallas kernels for 6%

commit v1 on v0

--- a/solution.py
+++ b/solution.py
@@ -73,30 +73,20 @@
     pltpu.make_async_copy(view, view, sem).wait()
 
 
-def reach_all(step_map, doublings):
-    total = None
-    power = step_map
-    for index in range(doublings):
-        if total is None:
-            n = step_map.shape[0]
-            eye = lax.broadcasted_iota(jnp.int32, (n, n), 0) == lax.broadcasted_iota(
-                jnp.int32, (n, n), 1
-            )
-            total = jnp.where(eye, 1.0, 0.0) + power
-        else:
-            total = total + dot_nn(total.astype(bf16), power.astype(bf16))
-        if index < doublings - 1:
-            power = dot_nn(power.astype(bf16), power.astype(bf16))
-    return total
-
-
 def split_colors(src_partner, dst_partner, doublings):
     n = src_partner.shape[0]
     row = lax.broadcasted_iota(jnp.int32, (n, n), 0)
     col = lax.broadcasted_iota(jnp.int32, (n, n), 1)
-    src_f = jnp.where(src_partner, 1.0, 0.0)
-    dst_f = jnp.where(dst_partner, 1.0, 0.0)
-    orbit = reach_all(dot_nn(src_f.astype(bf16), dst_f.astype(bf16)), doublings) > 0.5
+    src_b = jnp.where(src_partner, 1.0, 0.0).astype(bf16)
+    dst_b = jnp.where(dst_partner, 1.0, 0.0).astype(bf16)
+    power = dot_nn(src_b, dst_b).astype(bf16)
+    total = jnp.where(row == col, 1.0, 0.0) + power.astype(f32)
+    yield
+    for _ in range(doublings - 1):
+        power = dot_nn(power, power).astype(bf16)
+        total = total + dot_nn(total.astype(bf16), power)
+        yield
+    orbit = total > 0.5
     lead_c = jnp.min(jnp.where(orbit, col, n), axis=1, keepdims=True)
     lead_r = jnp.min(jnp.where(orbit, row, n), axis=0, keepdims=True)
     other_c = jnp.sum(jnp.where(src_partner, lead_r, 0), axis=1, keepdims=True)
@@ -117,16 +107,19 @@
     rank_r = jnp.sum(jnp.where(dst_same & (row < col), 1, 0), axis=0, keepdims=True)
     src_partner = col == (row ^ 2)
     dst_partner = dst_same & (rank_r == (rank_c ^ 1))
-    one_c, one_r = split_colors(src_partner, dst_partner, 5)
+    yield
+    one_c, one_r = yield from split_colors(src_partner, dst_partner, 5)
+    yield
     alike = (one_c == one_r) & (row != col)
-    two_c, _ = split_colors(src_same & alike, dst_same & alike, 4)
+    two_c, _ = yield from split_colors(src_same & alike, dst_same & alike, 4)
+    yield
     color = jnp.broadcast_to(2 * one_c + two_c, (n, n))
     src = row >> 3
     pair = (row & 7) >> 1
     half = row & 1
     even = half == 0
     mine = src == me
-    turn = me >> 2
+    turn = me // 4
 
     def pick(mask, value):
         return jnp.sum(jnp.where(mask, value, 0), axis=0, keepdims=True)
@@ -143,48 +136,218 @@
     return jnp.concatenate(rows, axis=0)
 
 
-def tables_kernel(dest_ref, tab_ref, every, send_sem, recv_sem):
-    me = lax.axis_index("seq")
-    greet("seq", PEERS, me)
-
-    def body(step, carry):
-        peer = lax.rem(me + step, PEERS)
-        pltpu.make_async_remote_copy(
-            src_ref=dest_ref,
-            dst_ref=every.at[me],
-            send_sem=send_sem,
-            recv_sem=recv_sem,
-            device_id={"seq": peer},
-            device_id_type=MESH,
-        ).start()
-        return carry
-
-    lax.fori_loop(1, PEERS, body, 0)
-    every[me] = dest_ref[...]
-    wait_all(every, recv_sem)
-    wait_all(every, send_sem)
-    tab_ref[...] = color_tables(every[...].reshape(PEERS * 8, 128), me)
+PLANES = 8
+ROWS = 160
+PIECE = 256
+COLS = 4 * PIECE
+ARRIVALS = PLANES - 1
 
 
 def encoder_kernel(
-    tab_ref, image_ref, x_ref, gain_ref, qkv_ref, out_ref, kv_ref, pay_ref, normed, mixed, att, hidden
+    image_ref,
+    dest_ref,
+    x_hbm,
+    gain_ref,
+    qkv_hbm,
+    own_out_ref,
+    kv_hbm,
+    pay_ref,
+    tab_out_ref,
+    x_ref,
+    every,
+    tab_ref,
+    weight,
+    out_parts,
+    out_ref,
+    kv_ref,
+    normed,
+    mixed,
+    att,
+    hidden,
+    local_sem,
+    dest_sem,
+    own_sem,
+    kv_sem,
+    z_send,
+    z_recv,
+    o_send,
+    o_recv,
+    r_send,
+    r_recv,
+    m_send,
+    m_recv,
+    om_sem,
 ):
     tokens, vis = x_ref.shape
     span = 2 * BLK
-
-    def norm_rows(t, carry):
-        rows = pl.ds(pl.multiple_of(t * 64, 64), 64)
+    e, q, m = lax.axis_index("enc"), lax.axis_index("seq"), lax.axis_index("mp")
+    other = 1 - m
+    d = 1 - 2 * m
+    stride = 1 + 3 * m
+    pos = lax.rem(q // stride, 4)
+    ring = q - pos * stride
+    left, right = lax.rem(pos + 3, 4), lax.rem(pos + 1, 4)
+    ahead, behind = lax.rem(e + d + PLANES, PLANES), lax.rem(e - d + PLANES, PLANES)
+    to_left, to_right = {"seq": ring + left * stride}, {"seq": ring + right * stride}
+    to_ahead, to_behind, to_mate = {"enc": ahead}, {"enc": behind}, {"mp": other}
+
+    def plane_rows(plane):
+        return pl.ds(pl.multiple_of(plane * ROWS, ROWS), ROWS)
+
+    def columns(at, count):
+        return pl.ds(pl.multiple_of(at, HEAD), count)
+
+    def remote(source, target, send, recv, device):
+        copy = pltpu.make_async_remote_copy(
+            src_ref=source,
+            dst_ref=target,
+            send_sem=send,
+            recv_sem=recv,
+            device_id=device,
+            device_id_type=MESH,
+        )
+        copy.start()
+
+    def done(view, sem):
+        pltpu.make_async_copy(view, view, sem).wait()
+
+    own_rows = pl.ds(pl.multiple_of(e * ROWS + m * (ROWS // 2), ROWS // 2), ROWS // 2)
+    kv_half = kv_hbm.shape[0]
+    kv_rows = pl.ds(pl.multiple_of(m * kv_half, kv_half), kv_half)
+    qkv_copy = pltpu.make_async_copy(
+        qkv_hbm, weight.at[own_rows, pl.ds(0, qkv_hbm.shape[1])], local_sem.at[0]
+    )
+    x_copy = pltpu.make_async_copy(x_hbm, x_ref, local_sem.at[1])
+    kv_copy = pltpu.make_async_copy(kv_hbm, kv_ref.at[kv_rows], local_sem.at[2])
+    qkv_copy.start()
+    x_copy.start()
+    kv_copy.start()
+    out_parts[m, e, 0 : own_out_ref.shape[0], :] = own_out_ref[...]
+
+    barrier = pltpu.get_barrier_semaphore()
+
+    def hello(step, carry):
+        pl.semaphore_signal(
+            barrier, inc=1, device_id={"seq": lax.rem(q + step, PEERS)}, device_id_type=MESH
+        )
+        return carry
+
+    lax.fori_loop(1, PEERS, hello, 0)
+    for device in (to_ahead, to_behind, to_mate):
+        pl.semaphore_signal(barrier, inc=1, device_id=device, device_id_type=MESH)
+    pl.semaphore_wait(barrier, PEERS + 2)
+
+    qkv_copy.wait()
+    for which, start in ((0, other), (1, m)):
+        view = weight.at[own_rows, columns(start * COLS, COLS)]
+        remote(view, view, own_sem.at[0, which], own_sem.at[1, which], to_mate)
+
+    def send_dest(step, carry):
+        peer = lax.rem(q + step, PEERS)
+        remote(dest_ref, every.at[q], dest_sem.at[0], dest_sem.at[1], {"seq": peer})
+        return carry
+
+    lax.fori_loop(1, PEERS, send_dest, 0)
+    every[q] = dest_ref[...]
+
+    mate_rows = pl.ds(
+        pl.multiple_of(e * ROWS + other * (ROWS // 2), ROWS // 2), ROWS // 2
+    )
+    done(weight.at[mate_rows, columns(m * COLS, COLS)], own_sem.at[1, 0])
+
+    my_cols = columns(m * COLS + pos * PIECE, PIECE)
+
+    def send_z(plane, arrival, device):
+        view = weight.at[plane_rows(plane), my_cols]
+        remote(view, view, z_send.at[arrival], z_recv.at[arrival], device)
+
+    def send_out(plane, arrival, device):
+        view = out_parts.at[m, plane]
+        remote(view, view, o_send.at[arrival], o_recv.at[arrival], device)
+
+    for send in (send_z, send_out):
+        send(e, 0, to_ahead)
+        send(e, 1, to_behind)
+    kv_there = kv_ref.at[kv_rows]
+    remote(kv_hbm, kv_there, kv_sem.at[0], kv_sem.at[1], to_mate)
+    x_copy.wait()
+
+    def norm_rows(t):
+        rows = slice(t * 64, t * 64 + 64)
         values = x_ref[rows, :].astype(f32)
         center = values - jnp.mean(values, axis=-1, keepdims=True)
         spread = jnp.mean(center * center, axis=-1, keepdims=True)
         normed[rows, :] = (center * lax.rsqrt(spread + EPS) * gain_ref[...]).astype(bf16)
-        return carry
-
-    lax.fori_loop(0, tokens // 64, norm_rows, 0)
+
+    def jobs():
+        for t in range(2):
+            norm_rows(t)
+            yield
+        wait_all(every, dest_sem.at[1])
+        tab_out_ref[...] = yield from color_tables(every[...].reshape(PEERS * 8, 128), q)
+        yield
+        for t in range(2, tokens // 64):
+            norm_rows(t)
+            yield
+
+    work = jobs()
+
+    def plane_of(arrival):
+        hops = arrival // 2 + 1
+        if arrival % 2 == 0:
+            return lax.rem(e - d * hops + PLANES, PLANES)
+        return lax.rem(e + d * hops + PLANES, PLANES)
+
+    def piece(k, place):
+        return weight.at[plane_rows(plane_of(k)), columns(m * COLS + place * PIECE, PIECE)]
+
+    def part(k, place, which):
+        return weight.at[
+            plane_rows(plane_of(k)),
+            columns(m * COLS + place * PIECE + which * (PIECE // 2), PIECE // 2),
+        ]
+
+    far = lax.rem(pos + 2, 4)
+    for k in range(ARRIVALS + 2):
+        if k < ARRIVALS:
+            device = to_ahead if k % 2 == 0 else to_behind
+            plane = plane_of(k)
+            done(piece(k, pos), z_recv.at[k])
+            if k + 2 < ARRIVALS:
+                send_z(plane, k + 2, device)
+            remote(piece(k, pos), piece(k, pos), r_send.at[k, 0], r_recv.at[k, 0], to_right)
+            remote(piece(k, pos), piece(k, pos), r_send.at[k, 1], r_recv.at[k, 1], to_left)
+            done(out_parts.at[m, plane], o_recv.at[k])
+            if k + 2 < ARRIVALS:
+                send_out(plane, k + 2, device)
+        j = k - 1
+        if 0 <= j < ARRIVALS:
+            done(piece(j, left), r_recv.at[j, 0])
+            remote(part(j, left, 0), part(j, left, 0), r_send.at[j, 2], r_recv.at[j, 2], to_right)
+            done(piece(j, right), r_recv.at[j, 1])
+            remote(part(j, right, 1), part(j, right, 1), r_send.at[j, 3], r_recv.at[j, 3], to_left)
+        j = k - 2
+        if 0 <= j < ARRIVALS:
+            done(part(j, far, 0), r_recv.at[j, 2])
+            done(part(j, far, 1), r_recv.at[j, 3])
+            view = weight.at[plane_rows(plane_of(j)), columns(m * COLS, COLS)]
+            remote(view, view, m_send.at[j], m_recv.at[j], to_mate)
+        if k == ARRIVALS - 1:
+            remote(out_parts.at[m], out_parts.at[m], om_sem.at[0], om_sem.at[1], to_mate)
+        for _ in range(3):
+            next(work, None)
+    for _ in work:
+        pass
+    tab_copy = pltpu.make_async_copy(tab_out_ref, tab_ref, local_sem.at[3])
+    tab_copy.start()
+
+    done(weight.at[mate_rows, columns(other * COLS, COLS)], own_sem.at[1, 1])
+    for k in range(ARRIVALS):
+        done(weight.at[plane_rows(e), columns(0, COLS)], m_recv.at[k])
 
     def mix_columns(t, carry):
         cols = pl.ds(pl.multiple_of(t * 384, 128), 384)
-        mixed[:, cols] = dot_nn(normed[...], qkv_ref[:, cols]).astype(bf16)
+        mixed[:, cols] = dot_nn(normed[...], weight[:, cols]).astype(bf16)
         return carry
 
     lax.fori_loop(0, mixed.shape[1] // 384, mix_columns, 0)
@@ -206,47 +369,70 @@
             base = first * 128
             lane = lax.broadcasted_iota(jnp.int32, (span, cut), 1) + base
             inside = (lane >= head * VHEAD) & (lane < (head + 1) * VHEAD)
-            q = jnp.where(inside, mixed[rows, base : base + cut], jnp.zeros((), bf16))
-            k = mixed[rows, width + base : width + base + cut]
-            v = mixed[rows, 2 * width + base : 2 * width + base + cut]
-            scores = jnp.where(allowed, dot_nt(k, q) * scale, -jnp.inf)
+            query = jnp.where(inside, mixed[rows, base : base + cut], jnp.zeros((), bf16))
+            key = mixed[rows, width + base : width + base + cut]
+            value = mixed[rows, 2 * width + base : 2 * width + base + cut]
+            scores = jnp.where(allowed, dot_nt(key, query) * scale, -jnp.inf)
             terms = jnp.exp(scores - jnp.max(scores, axis=0, keepdims=True))
             weights = (terms / jnp.sum(terms, axis=0, keepdims=True)).astype(bf16)
-            result = dot_tn(weights, v)
+            result = dot_tn(weights, value)
             for tile in range(first, last + 1):
                 at = (tile - first) * 128
-                part = result[:, at : at + 128]
+                found = result[:, at : at + 128]
                 if tiles[tile] is None:
-                    tiles[tile] = part
+                    tiles[tile] = found
                 else:
-                    tiles[tile] = jnp.where(inside[:, at : at + 128], part, tiles[tile])
+                    tiles[tile] = jnp.where(inside[:, at : at + 128], found, tiles[tile])
         att[rows, :] = jnp.concatenate(tiles, axis=1).astype(bf16)
         return carry
 
     lax.fori_loop(0, tokens // span, attend, 0)
+
+    done(out_parts.at[other], om_sem.at[1])
+    have = own_out_ref.shape[0]
+    for plane in range(PLANES):
+        both = [out_parts[core, plane, 0:have, :].astype(f32) for core in range(2)]
+        out_ref[2 * have * plane : 2 * have * (plane + 1), :] = jnp.concatenate(
+            both, axis=0
+        ).astype(bf16)
 
     def project(t, carry):
         cols = pl.ds(pl.multiple_of(t * 256, 256), 256)
-        part = x_ref[:, cols].astype(f32) + dot_nn(att[...], out_ref[:, cols])
-        hidden[:, :, cols] = part.astype(bf16).reshape(PAIRS, span, 256)
+        total = x_ref[:, cols].astype(f32) + dot_nn(att[...], out_ref[:, cols])
+        hidden[:, :, cols] = total.astype(bf16).reshape(PAIRS, span, 256)
         return carry
 
     lax.fori_loop(0, vis // 256, project, 0)
 
+    tab_copy.wait()
+    kv_copy.wait()
+    done(kv_there, kv_sem.at[1])
     half = KVHEADS * HEAD
-    for piece in range(PIECES):
+    for h in range(PIECES):
 
         def make_pay(t, carry):
-            source = jnp.concatenate([hidden[tab_ref[0, c]] for c in range(PAIRS)], axis=0)
-            at = pl.multiple_of((piece * PER + t) * HEAD, HEAD)
-            weight = jnp.concatenate(
+            source = jnp.concatenate([hidden[tab_ref[0, c] & 3] for c in range(PAIRS)], axis=0)
+            at = pl.multiple_of((h * PER + t) * HEAD, HEAD)
+            both = jnp.concatenate(
                 [kv_ref[:, pl.ds(at, HEAD)], kv_ref[:, pl.ds(half + at, HEAD)]], axis=1
             )
-            got = dot_nn(source, weight).astype(bf16).reshape(PEERS, span // 4, 2 * HEAD)
-            pay_ref[piece, :, :, pl.ds(pl.multiple_of(t * 2 * HEAD, 2 * HEAD), 2 * HEAD)] = got
+            got = dot_nn(source, both).astype(bf16).reshape(PEERS, span // 4, 2 * HEAD)
+            pay_ref[h, :, :, pl.ds(pl.multiple_of(t * 2 * HEAD, 2 * HEAD), 2 * HEAD)] = got
             return carry
 
         lax.fori_loop(0, PER, make_pay, 0)
+
+    wait_all(every, dest_sem.at[0])
+    for which, start in ((0, other), (1, m)):
+        done(weight.at[own_rows, columns(start * COLS, COLS)], own_sem.at[0, which])
+    done(kv_there, kv_sem.at[0])
+    done(out_parts.at[m], om_sem.at[0])
+    for k in range(ARRIVALS):
+        done(piece(k, pos), z_send.at[k])
+        done(out_parts.at[m, e], o_send.at[k])
+        for way in range(4):
+            done(piece(k, pos) if way < 2 else part(k, pos, 0), r_send.at[k, way])
+        done(weight.at[plane_rows(e), columns(0, COLS)], m_send.at[k])
 
 
 def cross_kernel(
@@ -294,7 +480,7 @@
         wait_all(got[h], recv_sem.at[phase - 1, h])
 
         def body(d, carry):
-            out[h][d] = got[h][tab_ref[row, d]]
+            out[h][d] = got[h][tab_ref[row, d] & 15]
             return carry
 
         lax.fori_loop(0, PEERS, body, 0)
@@ -307,7 +493,7 @@
         seen = seen_ref[pl.ds(s, 1), :]
         for kb in range(CAP):
             index = tab_ref[4, s * CAP + kb]
-            block = got2[h][pl.ds(2 * jnp.maximum(index, 0), 2), :, pl.ds(at, 2 * HEAD)]
+            block = got2[h][pl.ds(2 * (jnp.maximum(index, 0) & 7), 2), :, pl.ds(at, 2 * HEAD)]
             blocks.append(
                 jnp.where(index >= 0, block, jnp.zeros((), bf16)).reshape(BLK, 2 * HEAD)
             )
@@ -356,7 +542,7 @@
         lax.fori_loop(0, PER * CAP // 2, body, 0)
 
         def pack(cb, carry):
-            block = gkv[tab_ref[5, cb]]
+            block = gkv[tab_ref[5, cb] & 15]
             out3[h][pl.ds(2 * cb, 2)] = block.reshape(2, BLK // 2, WIDE)
             return carry
 
@@ -374,7 +560,7 @@
     for h in range(PIECES):
         wait_all(got4[h], recv_sem.at[3, h])
         for j in range(PAIRS):
-            color = tab_ref[1, j]
+            color = tab_ref[1, j] & 3
             block = got4[h][pl.ds(4 * color, 4)].reshape(2, BLK, WIDE)
             for gi in range(PER):
                 at = (h * PER + gi) * HEAD
@@ -391,6 +577,7 @@
 
 VMEM = pl.BlockSpec(memory_space=pltpu.VMEM)
 SMEM = pl.BlockSpec(memory_space=pltpu.SMEM)
+ANY = pl.BlockSpec(memory_space=pl.ANY)
 LIMIT = 48 * 1024 * 1024
 
 
@@ -411,42 +598,47 @@
 ):
     enc_blocks, block_len, vis = images.shape
     tokens = enc_blocks * block_len
-    full_qkv = lax.all_gather(vit_qkv, ("enc", "mp"), axis=0, tiled=True)
-    full_out = lax.all_gather(vit_out, ("enc", "mp"), axis=0, tiled=True)
-    full_kv = lax.all_gather(kv_weight, "mp", axis=0, tiled=True)
-    tables = pl.pallas_call(
-        tables_kernel,
-        out_shape=jax.ShapeDtypeStruct((8, 128), jnp.int32),
-        in_specs=[VMEM],
-        out_specs=VMEM,
+    slots = (PIECES, PEERS, BLK // 2, WIDE)
+    payload, tables = pl.pallas_call(
+        encoder_kernel,
+        out_shape=(
+            jax.ShapeDtypeStruct(slots, bf16),
+            jax.ShapeDtypeStruct((8, 128), jnp.int32),
+        ),
+        in_specs=[SMEM, VMEM, ANY, VMEM, ANY, VMEM, ANY],
+        out_specs=(VMEM, VMEM),
         scratch_shapes=[
+            pltpu.VMEM((tokens, vis), bf16),
             pltpu.VMEM((PEERS, 8, 128), jnp.int32),
-            pltpu.SemaphoreType.DMA,
-            pltpu.SemaphoreType.DMA,
-        ],
-        compiler_params=pltpu.CompilerParams(collective_id=0, has_side_effects=True),
-    )(jnp.broadcast_to(block_dest[:, None], (8, 128)))
-    slots = (PIECES, PEERS, BLK // 2, WIDE)
-    payload = pl.pallas_call(
-        encoder_kernel,
-        out_shape=jax.ShapeDtypeStruct(slots, bf16),
-        in_specs=[SMEM, SMEM] + [VMEM] * 5,
-        out_specs=VMEM,
-        scratch_shapes=[
+            pltpu.SMEM((8, 128), jnp.int32),
+            pltpu.VMEM((vis, 2 * COLS), bf16),
+            pltpu.VMEM((2, PLANES, 48, vis), bf16),
+            pltpu.VMEM((VHEADS * VHEAD, vis), bf16),
+            pltpu.VMEM((vis, 2 * KVHEADS * HEAD), bf16),
             pltpu.VMEM((tokens, vis), bf16),
             pltpu.VMEM((tokens, 3 * VHEADS * VHEAD), bf16),
             pltpu.VMEM((tokens, VHEADS * VHEAD), bf16),
             pltpu.VMEM((PAIRS, 2 * BLK, vis), bf16),
-        ],
-        compiler_params=pltpu.CompilerParams(vmem_limit_bytes=LIMIT),
+            pltpu.SemaphoreType.DMA((4,)),
+            pltpu.SemaphoreType.DMA((2,)),
+            pltpu.SemaphoreType.DMA((2, 2)),
+            pltpu.SemaphoreType.DMA((2,)),
+        ]
+        + [pltpu.SemaphoreType.DMA((ARRIVALS,))] * 4
+        + [pltpu.SemaphoreType.DMA((ARRIVALS, 4))] * 2
+        + [pltpu.SemaphoreType.DMA((ARRIVALS,))] * 2
+        + [pltpu.SemaphoreType.DMA((2,))],
+        compiler_params=pltpu.CompilerParams(
+            collective_id=0, has_side_effects=True, vmem_limit_bytes=LIMIT
+        ),
     )(
-        tables,
         block_image,
+        jnp.broadcast_to(block_dest[:, None], (8, 128)),
         images.reshape(tokens, vis),
         vit_gain.reshape(1, vis),
-        full_qkv,
-        full_out,
-        full_kv,
+        vit_qkv,
+        vit_out,
+        kv_weight,
     )
     seen = jnp.tile(text_seen.reshape(CAP, 1, LEN), (1, SHARED, 1)).reshape(CAP, SHARED * LEN)
     attended, kv_grad = pl.pallas_call(

time: 206 us -> 122 us (0.59)
  waiting for transfers between devices: 93.8 us -> 0 us
  Pallas kernels: 92.8 us -> 110 us
  between operations: 13.9 us -> 0.71 us
  local copies, waits for them, and re-layouts: 4.93 us -> 9.35 us
    all_gather x3 -> x0, waiting for transfers between devices: 91.7 us -> none  [the longest x1 43.7 us: local(): full_qkv = lax.all_gather(vit_qkv, ('enc', 'mp'), axis=0, tiled=True)]
    pallas_call x2 -> x1, Pallas kernels: 32.8 us -> 54.6 us  [local(): pl.pallas_call(encoder_kernel, out_shape=(jax.ShapeDtypeStruct(slots, bf1...]
    pallas_call x1, Pallas kernels: 59.9 us -> 55.8 us  [local(): pl.pallas_call(cross_kernel, out_shape=(jax.ShapeDtypeStruct(queries.shap...]
    unnamed x26 -> x22, local copies, waits for them, and re-layouts: 4.09 us -> 7.11 us
  transfers between devices with their start and end apart: 3 -> 0, of which waited for: 3 -> 0; matrix products, arithmetic and copies ran while one was open for 0% -> 0% of each run, Pallas kernels for 6% -> 0%
where the time goes in v1:
time: 122 us; the launch traced here: 120 us
  Pallas kernels  110 us (90%)
  local copies, waits for them, and re-layouts  9.35 us (8%)
    pallas_call x1, Pallas kernels, local(): pl.pallas_call(cross_kernel, out_shape=(jax.ShapeDtypeStruct(queries.shap...  55.8 us
    pallas_call x1, Pallas kernels, local(): pl.pallas_call(encoder_kernel, out_shape=(jax.ShapeDtypeStruct(slots, bf1...  54.6 us
    unnamed x22, local copies, waits for them, and re-layouts  7.11 us

profile of v1, /device:TPU:32, one launch (start us, length us, event | category | flops | bytes accessed | tf_op | source)
XLA Modules:
  0.0 120.4 jit_solution(6993977221958473645)
XLA Ops:
  0.6 0.7 tile.9
  1.4 0.7 broadcast_in_dim.2.dest_ref
  2.1 0.7 reshape.22.gain_ref
  2.8 0.1 tile.11.seen_ref
  2.9 0.0 copy-start
  2.9 1.3 %copy-done = bf16[8,64,1280]{2,1,0:T(8,128)(2,1)S(1)} copy-done((bf16[8,64,1280]{2,1,0:T(8,128)(2,1)S(1)}, bf16[8,64,1280]{2,1,0:T(8,128)(2,1)}, u32[]{:S(2)}) %copy-start) | copy-done | bytes 1310744
  4.2 0.0 copy-start.1
  4.2 1.3 %copy-done.1 = bf16[640,1024]{1,0:T(8,128)(2,1)S(1)} copy-done((bf16[640,1024]{1,0:T(8,128)(2,1)S(1)}, bf16[640,1024]{1,0:T(8,128)(2,1)}, u32[]{:S(2)}) %copy-start.1) | copy-done | bytes 1310744
  5.5 0.0 copy-start.4
  5.5 1.0 copy-done.4
  6.5 0.0 copy-start.5
  6.5 0.9 copy-done.5
  7.4 0.0 copy-start.7
  7.4 0.7 copy-done.7
  8.0 0.0 copy-start.2
  8.0 0.0 copy-start.3
  8.0 0.0 copy-start.6
  8.0 0.0 copy-start.8
  8.0 0.0 copy-start.9
  8.1 54.6 %shard_map.140 = (bf16[2,16,32,512]{3,2,1,0:T(8,128)(2,1)S(1)}, s32[8,128]{1,0:T(8,128)S(1)}) custom-call(s32[8]{0:T(128)S(1)} %copy-done.7, s32[8,128]{1,0:T(8,128)S(1)} %broadcast_in_dim.2.dest_ref, bf16[512,1280]{1,0:T(8,128)(2,1)S(1)} %bitcast.7, f32[1,1280]{1,0:T(1,128)S(1)} %reshape.22.gain_ref, bf16[80,1920]{1,0:T(8,128)(2,1)S(1)} %copy-done.4, ...), custom_call_target="tpu_custom_call" | custom-call | tf_op jit(solution)/shard_map/pallas_call | solution.py:602
  62.6 0.0 copy-done.2
  62.6 0.0 copy-done.3
  62.6 0.0 copy-done.6
  62.6 0.0 copy-done.8
  62.7 0.0 copy-done.9
  62.7 55.8 %shard_map.141 = (bf16[128,4096]{1,0:T(8,128)(2,1)S(1)}, bf16[8,64,1024]{2,1,0:T(8,128)(2,1)S(1)}) custom-call(s32[8,128]{1,0:T(8,128)S(1)} %get-tuple-element.4.tab_ref, s32[4,4]{1,0:T(4,128)S(1)} %copy-done.6, s32[4,256]{1,0:T(4,128)S(1)} %tile.11.seen_ref, bf16[2,16,32,512]{3,2,1,0:T(8,128)(2,1)S(1)} %get-tuple-element.5.pay_ref, ...), custom_call_target="tpu_custom_call" | custom-call | tf_op jit(solution)/shard_map/pallas_call | solution.py:644
  118.4 1.0 copy.17
  119.4 1.0 copy.18
  (1 shorter events, 0.0 us)
Async XLA Ops:
  2.9 1.3 %copy-start = (bf16[8,64,1280]{2,1,0:T(8,128)(2,1)S(1)}, bf16[8,64,1280]{2,1,0:T(8,128)(2,1)}, u32[]{:S(2)}) copy-start(bf16[8,64,1280]{2,1,0:T(8,128)(2,1)} %param.13) | copy-start | bytes 3932164
  4.2 1.3 %copy-start.1 = (bf16[640,1024]{1,0:T(8,128)(2,1)S(1)}, bf16[640,1024]{1,0:T(8,128)(2,1)}, u32[]{:S(2)}) copy-start(bf16[640,1024]{1,0:T(8,128)(2,1)} %kv_hbm.1) | copy-start | bytes 3932164
  5.5 1.0 copy-start.4
  6.5 0.9 copy-start.5
  7.4 0.7 copy-start.7
  8.0 54.6 %copy-start.2 = (bf16[128,4096]{1,0:T(8,128)(2,1)S(1)}, bf16[128,4096]{1,0:T(8,128)(2,1)}, u32[]{:S(2)}) copy-start(bf16[128,4096]{1,0:T(8,128)(2,1)} %q_ref.1) | copy-start | bytes 3145732
  8.0 54.6 %copy-start.3 = (bf16[128,4096]{1,0:T(8,128)(2,1)S(1)}, bf16[128,4096]{1,0:T(8,128)(2,1)}, u32[]{:S(2)}) copy-start(bf16[128,4096]{1,0:T(8,128)(2,1)} %og_ref.1) | copy-start | bytes 3145732
  8.0 54.6 %copy-start.6 = (s32[4,4]{1,0:T(4,128)S(1)}, s32[4,4]{1,0:T(4,128)}, u32[]{:S(2)}) copy-start(s32[4,4]{1,0:T(4,128)} %kimg_ref.1) | copy-start | bytes 196
  8.0 54.6 %copy-start.8 = (f32[128]{0:T(128)S(1)}, f32[128]{0:T(128)}, u32[]{:S(2)}) copy-start(f32[128]{0:T(128)} %param.19) | copy-start | bytes 1540
  8.0 54.6 %copy-start.9 = (f32[128]{0:T(128)S(1)}, f32[128]{0:T(128)}, u32[]{:S(2)}) copy-start(f32[128]{0:T(128)} %param.20) | copy-start | bytes 1540

commit v2 on v1

v2 whole, which is shorter than its diff:
```python
import math

import jax
import jax.numpy as jnp
from jax import lax
from jax.experimental import pallas as pl
from jax.experimental.pallas import tpu as pltpu
from jax.sharding import PartitionSpec as P

VHEADS = 8
VHEAD = 80
HEAD = 128
KVHEADS = 4
SHARED = 8
BLK = 64
LEN = 32
CAP = 4
PEERS = 16
PAIRS = 4
PIECES = 4
PER = KVHEADS // PIECES
WIDE = PER * 2 * HEAD
EPS = 1e-05
MESH = pl.DeviceIdType.MESH
f32 = jnp.float32
bf16 = jnp.bfloat16


def dot_nn(left, right):
    return jnp.dot(left, right, preferred_element_type=f32)


def dot_nt(left, right):
    return lax.dot_general(left, right, (((1,), (1,)), ((), ())), preferred_element_type=f32)


def dot_tn(left, right):
    return lax.dot_general(left, right, (((0,), (0,)), ((), ())), preferred_element_type=f32)


def exchange(source, target, me, send_sem, recv_sem):
    def body(step, carry):
        peer = lax.rem(me + step, PEERS)
        pltpu.make_async_remote_copy(
            src_ref=source.at[peer],
            dst_ref=target.at[me],
            send_sem=send_sem,
            recv_sem=recv_sem,
            device_id={"seq": peer},
            device_id_type=MESH,
        ).start()
        return carry

    lax.fori_loop(1, PEERS, body, 0)
    target[me] = source[me]


def wait_all(buffer, sem):
    view = buffer.at[pl.ds(0, PEERS - 1)]
    pltpu.make_async_copy(view, view, sem).wait()


def split_colors(src_partner, dst_partner, doublings):
    n = src_partner.shape[0]
    row = lax.broadcasted_iota(jnp.int32, (n, n), 0)
    col = lax.broadcasted_iota(jnp.int32, (n, n), 1)
    src_b = jnp.where(src_partner, 1.0, 0.0).astype(bf16)
    dst_b = jnp.where(dst_partner, 1.0, 0.0).astype(bf16)
    power = dot_nn(src_b, dst_b).astype(bf16)
    total = jnp.where(row == col, 1.0, 0.0) + power.astype(f32)
    yield
    for _ in range(doublings - 1):
        power = dot_nn(power, power).astype(bf16)
        total = total + dot_nn(total.astype(bf16), power)
        yield
    orbit = total > 0.5
    lead_c = jnp.min(jnp.where(orbit, col, n), axis=1, keepdims=True)
    lead_r = jnp.min(jnp.where(orbit, row, n), axis=0, keepdims=True)
    other_c = jnp.sum(jnp.where(src_partner, lead_r, 0), axis=1, keepdims=True)
    other_r = jnp.sum(jnp.where(src_partner, lead_c, 0), axis=0, keepdims=True)
    return (lead_c < other_c).astype(jnp.int32), (lead_r < other_r).astype(jnp.int32)


def color_tables(dest, me):
    n = dest.shape[0]
    row = lax.broadcasted_iota(jnp.int32, (n, n), 0)
    col = lax.broadcasted_iota(jnp.int32, (n, n), 1)
    dest_t = jnp.transpose(dest.astype(f32)).astype(jnp.int32)
    owner_c, owner_r = dest >> 4, dest_t >> 4
    parity_same = (row & 1) == (col & 1)
    src_same = ((row >> 3) == (col >> 3)) & parity_same
    dst_same = (owner_c == owner_r) & parity_same
    rank_c = jnp.sum(jnp.where(dst_same & (col < row), 1, 0), axis=1, keepdims=True)
    rank_r = jnp.sum(jnp.where(dst_same & (row < col), 1, 0), axis=0, keepdims=True)
    src_partner = col == (row ^ 2)
    dst_partner = dst_same & (rank_r == (rank_c ^ 1))
    yield
    one_c, one_r = yield from split_colors(src_partner, dst_partner, 5)
    yield
    alike = (one_c == one_r) & (row != col)
    two_c, _ = yield from split_colors(src_same & alike, dst_same & alike, 4)
    yield
    color = jnp.broadcast_to(2 * one_c + two_c, (n, n))
    src = row >> 3
    pair = (row & 7) >> 1
    half = row & 1
    even = half == 0
    mine = src == me
    turn = me // 4

    def pick(mask, value):
        return jnp.sum(jnp.where(mask, value, 0), axis=0, keepdims=True)

    rows = [
        pick(mine & even & (color == col), pair),
        pick(mine & even & (pair == col), color),
        pick(even & (color == turn) & (owner_c == col), src),
        pick(even & (color == turn) & (src == col), owner_c),
        pick((owner_c == me) & ((dest & 15) == col), 2 * color + half + 1) - 1,
        pick((owner_c == me) & (2 * color + half == col), dest & 15),
    ]
    rows += [jnp.zeros_like(rows[0])] * 2
    return jnp.concatenate(rows, axis=0)


PLANES = 8
ROWS = 160
PIECE = 256
COLS = 4 * PIECE
ARRIVALS = PLANES - 1
CHUNK = 384
LOG2E = 1.4426950408889634


def softmax_over_rows(scores, allowed, scale):
    masked = jnp.where(allowed, scores, -jnp.inf)
    top = jnp.max(masked, axis=0, keepdims=True)
    terms = jnp.exp2((masked - top) * (scale * LOG2E))
    return terms * (1.0 / jnp.sum(terms, axis=0, keepdims=True))


def kernel(
    image_ref,
    dest_ref,
    kimg_ref,
    seen_ref,
    gain_ref,
    qg_ref,
    kg_ref,
    x_hbm,
    qkv_hbm,
    out_hbm,
    kv_hbm,
    q_hbm,
    og_hbm,
    att_ref,
    kvg_ref,
    x_ref,
    own_out,
    q_ref,
    og_ref,
    dest_tile,
    every,
    tab_tile,
    tab_ref,
    seen_rows,
    weight,
    out_parts,
    out_ref,
    kv_ref,
    normed,
    summed,
    mixed,
    att,
    hidden,
    pay,
    qn,
    gkv,
    got1,
    out2,
    got2,
    out3,
    got3,
    out4,
    got4,
    local_sem,
    dest_sem,
    own_sem,
    kv_sem,
    z_send,
    z_recv,
    o_send,
    o_recv,
    r_send,
    r_recv,
    m_send,
    m_recv,
    om_sem,
    send_sem,
    recv_sem,
):
    tokens, vis = x_ref.shape
    span = 2 * BLK
    e, q, m = lax.axis_index("enc"), lax.axis_index("seq"), lax.axis_index("mp")
    other = 1 - m
    d = 1 - 2 * m
    stride = 1 + 3 * m
    pos = lax.rem(q // stride, 4)
    ring = q - pos * stride
    left, right, far = lax.rem(pos + 3, 4), lax.rem(pos + 1, 4), lax.rem(pos + 2, 4)
    ahead, behind = lax.rem(e + d + PLANES, PLANES), lax.rem(e - d + PLANES, PLANES)
    to_left, to_right = {"seq": ring + left * stride}, {"seq": ring + right * stride}
    to_ahead, to_behind, to_mate = {"enc": ahead}, {"enc": behind}, {"mp": other}

    def plane_rows(plane):
        return pl.ds(pl.multiple_of(plane * ROWS, ROWS), ROWS)

    def columns(at, count):
        return pl.ds(pl.multiple_of(at, HEAD), count)

    def remote(source, target, send, recv, device):
        pltpu.make_async_remote_copy(
            src_ref=source,
            dst_ref=target,
            send_sem=send,
            recv_sem=recv,
            device_id=device,
            device_id_type=MESH,
        ).start()

    def done(view, sem):
        pltpu.make_async_copy(view, view, sem).wait()

    half_rows = ROWS // 2
    own_rows = pl.ds(pl.multiple_of(e * ROWS + m * half_rows, half_rows), half_rows)
    mate_rows = pl.ds(pl.multiple_of(e * ROWS + other * half_rows, half_rows), half_rows)
    kv_half = kv_hbm.shape[0]
    kv_rows = pl.ds(pl.multiple_of(m * kv_half, kv_half), kv_half)
    copies = [
        pltpu.make_async_copy(source, target, local_sem.at[index])
        for index, (source, target) in enumerate(
            (
                (qkv_hbm, weight.at[own_rows, pl.ds(0, qkv_hbm.shape[1])]),
                (x_hbm, x_ref),
                (out_hbm, own_out),
                (kv_hbm, kv_ref.at[kv_rows]),
                (q_hbm, q_ref),
                (og_hbm, og_ref),
                (tab_tile, tab_ref),
            )
        )
    ]
    qkv_copy, x_copy, out_copy, kv_copy, q_copy, og_copy, tab_copy = copies
    for copy in copies[:-1]:
        copy.start()

    barrier = pltpu.get_barrier_semaphore()

    def hello(step, carry):
        pl.semaphore_signal(
            barrier, inc=1, device_id={"seq": lax.rem(q + step, PEERS)}, device_id_type=MESH
        )
        return carry

    lax.fori_loop(1, PEERS, hello, 0)
    for device in (to_ahead, to_behind, to_mate):
        pl.semaphore_signal(barrier, inc=1, device_id=device, device_id_type=MESH)

    sub = lax.broadcasted_iota(jnp.int32, (8, 128), 0)
    lane = lax.broadcasted_iota(jnp.int32, (8, 128), 1)
    tile = jnp.zeros((8, 128), jnp.int32)
    for block in range(8):
        tile = jnp.where(sub == block, dest_ref[block], tile)
    dest_tile[...] = tile
    every[q] = tile
    spread = jnp.where(lane // LEN == sub, seen_ref[...].astype(f32), 0.0).astype(bf16)
    wide = (128, SHARED * LEN)
    place = lax.rem(lax.broadcasted_iota(jnp.int32, wide, 0), LEN) == lax.rem(
        lax.broadcasted_iota(jnp.int32, wide, 1), LEN
    )
    seen_rows[...] = dot_nn(spread, jnp.where(place, 1.0, 0.0).astype(bf16)).astype(jnp.int32)
    gain = jnp.concatenate([gain_ref[t : t + 1, :] for t in range(vis // 128)], axis=1)
    out_copy.wait()
    out_parts[m, e, 0 : own_out.shape[0], :] = own_out[...]
    qkv_copy.wait()
    pl.semaphore_wait(barrier, PEERS + 2)

    my_cols = columns(m * COLS + pos * PIECE, PIECE)
    for which, start in ((0, other), (1, m)):
        view = weight.at[own_rows, columns(start * COLS, COLS)]
        remote(view, view, own_sem.at[0, which], own_sem.at[1, which], to_mate)
    view = weight.at[own_rows, my_cols]
    remote(view, view, z_send.at[0], z_recv.at[0], to_ahead)
    remote(view, view, z_send.at[1], z_recv.at[1], to_behind)

    def send_dest(step, carry):
        peer = lax.rem(q + step, PEERS)
        remote(dest_tile, every.at[q], dest_sem.at[0], dest_sem.at[1], {"seq": peer})
        return carry

    lax.fori_loop(1, PEERS, send_dest, 0)
    done(weight.at[mate_rows, columns(m * COLS, COLS)], own_sem.at[1, 0])
    view = weight.at[mate_rows, my_cols]
    remote(view, view, z_send.at[0], z_recv.at[0], to_ahead)
    remote(view, view, z_send.at[1], z_recv.at[1], to_behind)
    kv_there = kv_ref.at[kv_rows]
    remote(kv_hbm, kv_there, kv_sem.at[0], kv_sem.at[1], to_mate)

    def send_z(plane, arrival, device):
        view = weight.at[plane_rows(plane), my_cols]
        remote(view, view, z_send.at[arrival], z_recv.at[arrival], device)

    def send_out(plane, arrival, device):
        view = out_parts.at[m, plane]
        remote(view, view, o_send.at[arrival], o_recv.at[arrival], device)

    def plane_of(arrival):
        hops = arrival // 2 + 1
        if arrival % 2 == 0:
            return lax.rem(e - d * hops + PLANES, PLANES)
        return lax.rem(e + d * hops + PLANES, PLANES)

    def piece(k, place):
        return weight.at[plane_rows(plane_of(k)), columns(m * COLS + place * PIECE, PIECE)]

    def part(k, place, which):
        return weight.at[
            plane_rows(plane_of(k)),
            columns(m * COLS + place * PIECE + which * (PIECE // 2), PIECE // 2),
        ]

    def pass_out(arrivals):
        for k in arrivals:
            done(out_parts.at[m, plane_of(k)], o_recv.at[k])
            if k + 2 < ARRIVALS:
                send_out(plane_of(k), k + 2, to_ahead if k % 2 == 0 else to_behind)

    chunks = 3 * VHEADS * VHEAD // CHUNK

    def norm_jobs():
        x_copy.wait()
        for t in range(tokens // 64):
            rows = slice(t * 64, t * 64 + 64)
            values = x_ref[rows, :].astype(f32)
            center = values - jnp.mean(values, axis=-1, keepdims=True)
            spread = jnp.mean(center * center, axis=-1, keepdims=True)
            result = (center * lax.rsqrt(spread + EPS) * gain).astype(bf16)
            for plane in range(PLANES):
                normed[plane, rows, :] = result[:, plane * ROWS : (plane + 1) * ROWS]
            yield

    def table_jobs():
        wait_all(every, dest_sem.at[1])
        tab_tile[...] = yield from color_tables(every[...].reshape(PEERS * 8, 128), q)
        tab_copy.start()

    def add_plane(plane, mode, begin, end):
        def body(t, carry):
            cols = pl.ds(pl.multiple_of(t * CHUNK, 128), CHUNK)
            found = dot_nn(normed[plane], weight[plane_rows(plane), cols])
            if mode == 0:
                summed[:, cols] = found
            elif mode == 1:
                summed[:, cols] += found
            else:
                mixed[:, cols] = (summed[:, cols] + found).astype(bf16)
            return carry

        lax.fori_loop(begin, end, body, 0)

    def plane_jobs(k):
        if k < 0:
            done(weight.at[mate_rows, columns(other * COLS, COLS)], own_sem.at[1, 1])
            plane = e
        else:
            same = k ^ 1 if k < ARRIVALS - 1 else k
            done(weight.at[plane_rows(e), columns(0, COLS)], m_recv.at[same])
            plane = plane_of(k)
        mode = 0 if k < 0 else 1 if k < ARRIVALS - 1 else 2
        add_plane(plane, mode, 0, 2)
        yield
        add_plane(plane, mode, 2, chunks)
        yield

    queue = [norm_jobs(), table_jobs(), plane_jobs(-1)]

    def pump(steps):
        while queue and steps > 0:
            try:
                next(queue[0])
                steps -= 1
            except StopIteration:
                queue.pop(0)

    pump(2)
    for k in range(ARRIVALS + 2):
        if k < ARRIVALS:
            done(piece(k, pos), z_recv.at[k])
            if k + 2 < ARRIVALS:
                send_z(plane_of(k), k + 2, to_ahead if k % 2 == 0 else to_behind)
            view = piece(k, pos)
            remote(view, view, r_send.at[k, 0], r_recv.at[k, 0], to_right)
            remote(view, view, r_send.at[k, 1], r_recv.at[k, 1], to_left)
        pump(2)
        j = k - 1
        if 0 <= j < ARRIVALS:
            view = part(j, left, 0)
            done(piece(j, left), r_recv.at[j, 0])
            remote(view, view, r_send.at[j, 2], r_recv.at[j, 2], to_right)
            view = part(j, right, 1)
            done(piece(j, right), r_recv.at[j, 1])
            remote(view, view, r_send.at[j, 3], r_recv.at[j, 3], to_left)
        pump(1)
        j = k - 2
        if 0 <= j < ARRIVALS:
            done(part(j, far, 0), r_recv.at[j, 2])
            done(part(j, far, 1), r_recv.at[j, 3])
            view = weight.at[plane_rows(plane_of(j)), columns(m * COLS, COLS)]
            remote(view, view, m_send.at[j], m_recv.at[j], to_mate)
        if k == 1:
            send_out(e, 0, to_ahead)
            send_out(e, 1, to_behind)
        if k == 4:
            pass_out((0, 1))
        if k == 6:
            pass_out((2, 3))
        pump(1)
        if k >= 3:
            queue.append(plane_jobs(k - 3))
    pump(1000)
    pass_out((4, 5))
    queue.append(plane_jobs(ARRIVALS - 1))
    pump(1000)

    width = VHEADS * VHEAD
    row = lax.broadcasted_iota(jnp.int32, (span, span), 0)
    col = lax.broadcasted_iota(jnp.int32, (span, span), 1)
    near = (row // BLK) == (col // BLK)

    def window(head):
        first, last = head * VHEAD // 128, ((head + 1) * VHEAD - 1) // 128
        return first, last, first * 128, (last - first + 1) * 128

    def attend_pair(j, carry):
        rows = pl.ds(pl.multiple_of(j * span, span), span)
        allowed = near | (image_ref[2 * j] == image_ref[2 * j + 1])
        insides, scores = [], []
        for head in range(VHEADS):
            _, _, base, cut = window(head)
            lanes = lax.broadcasted_iota(jnp.int32, (span, cut), 1) + base
            inside = (lanes >= head * VHEAD) & (lanes < (head + 1) * VHEAD)
            query = jnp.where(inside, mixed[rows, base : base + cut], jnp.zeros((), bf16))
            key = mixed[rows, width + base : width + base + cut]
            insides.append(inside)
            scores.append(dot_nt(key, query))
        weights = [
            softmax_over_rows(found, allowed, 1.0 / math.sqrt(VHEAD)).astype(bf16)
            for found in scores
        ]
        tiles = [None] * (width // 128)
        for head in range(VHEADS):
            first, last, base, cut = window(head)
            value = mixed[rows, 2 * width + base : 2 * width + base + cut]
            result = dot_tn(weights[head], value)
            for t in range(first, last + 1):
                at = (t - first) * 128
                found = result[:, at : at + 128]
                if tiles[t] is not None:
                    found = jnp.where(insides[head][:, at : at + 128], found, tiles[t])
                tiles[t] = found
        att[rows, :] = jnp.concatenate(tiles, axis=1).astype(bf16)
        return carry

    lax.fori_loop(0, PAIRS // 2, attend_pair, 0)
    pass_out((6,))
    remote(out_parts.at[m], out_parts.at[m], om_sem.at[0], om_sem.at[1], to_mate)
    lax.fori_loop(PAIRS // 2, PAIRS, attend_pair, 0)

    done(out_parts.at[other], om_sem.at[1])
    have = own_out.shape[0]
    for plane in range(PLANES):
        both = [out_parts[core, plane, 0:have, :].astype(f32) for core in range(2)]
        out_ref[2 * have * plane : 2 * have * (plane + 1), :] = jnp.concatenate(
            both, axis=0
        ).astype(bf16)

    def project(t, carry):
        cols = pl.ds(pl.multiple_of(t * 256, 256), 256)
        total = x_ref[:, cols].astype(f32) + dot_nn(att[...], out_ref[:, cols])
        hidden[:, :, cols] = total.astype(bf16).reshape(PAIRS, span, 256)
        return carry

    lax.fori_loop(0, vis // 256, project, 0)

    tab_copy.wait()
    kv_copy.wait()
    done(kv_there, kv_sem.at[1])
    half = KVHEADS * HEAD
    for h in range(PIECES):
        source = jnp.concatenate([hidden[tab_ref[0, c] & 3] for c in range(PAIRS)], axis=0)
        for t in range(PER):
            at = (h * PER + t) * HEAD
            both = jnp.concatenate(
                [kv_ref[:, at : at + HEAD], kv_ref[:, half + at : half + at + HEAD]], axis=1
            )
            pay[h][:, :, t * 2 * HEAD : (t + 1) * 2 * HEAD] = (
                dot_nn(source, both).astype(bf16).reshape(PEERS, span // 4, 2 * HEAD)
            )
        exchange(pay[h], got1[h], q, send_sem.at[0, h], recv_sem.at[0, h])

    q_copy.wait()

    def norm_queries(g, carry):
        block = q_ref[:, pl.ds(pl.multiple_of(g * SHARED * HEAD, HEAD), SHARED * HEAD)]
        for hh in range(SHARED):
            x = block[:, hh * HEAD : (hh + 1) * HEAD].astype(f32)
            inv = lax.rsqrt(jnp.mean(x * x, axis=-1, keepdims=True) + EPS)
            y = (x * inv * qg_ref[...]).astype(bf16)
            for s in range(CAP):
                qn[g, s, hh * LEN : (hh + 1) * LEN, :] = y[s * LEN : (s + 1) * LEN, :]
        return carry

    lax.fori_loop(0, KVHEADS, norm_queries, 0)
    og_copy.wait()

    def relay(h, got, out, table, target, phase):
        wait_all(got[h], recv_sem.at[phase - 1, h])

        def body(index, carry):
            out[h][index] = got[h][tab_ref[table, index] & 15]
            return carry

        lax.fori_loop(0, PEERS, body, 0)
        exchange(out[h], target[h], q, send_sem.at[phase, h], recv_sem.at[phase, h])

    def one(h, gi, s):
        g = h * PER + gi
        at = pl.multiple_of(gi * 2 * HEAD, 2 * HEAD)
        blocks, masks = [], []
        seen = seen_rows[pl.ds(s, 1), :]
        for kb in range(CAP):
            index = tab_ref[4, s * CAP + kb]
            block = got2[h][pl.ds(2 * (jnp.maximum(index, 0) & 7), 2), :, pl.ds(at, 2 * HEAD)]
            blocks.append(
                jnp.where(index >= 0, block, jnp.zeros((), bf16)).reshape(BLK, 2 * HEAD)
            )
            masks.append(jnp.broadcast_to(kimg_ref[s, kb] < seen, (BLK, SHARED * LEN)))
        keyval = jnp.concatenate(blocks, axis=0)
        allowed = jnp.concatenate(masks, axis=0)
        keys = keyval[:, :HEAD].astype(f32)
        values = keyval[:, HEAD:]
        inv = lax.rsqrt(jnp.mean(keys * keys, axis=-1, keepdims=True) + EPS)
        kn = (keys * inv * kg_ref[...]).astype(bf16)
        queries = qn[g, s]
        rows = pl.ds(pl.multiple_of(s * LEN, LEN), LEN)
        cols = pl.ds(pl.multiple_of(g * SHARED * HEAD, SHARED * HEAD), SHARED * HEAD)
        grad_row = og_ref[rows, cols]
        grads = jnp.concatenate(
            [grad_row[:, hh * HEAD : (hh + 1) * HEAD] for hh in range(SHARED)], axis=0
        )
        scale = 1.0 / math.sqrt(HEAD)
        weights = softmax_over_rows(dot_nt(kn, queries), allowed, scale)
        rounded = weights.astype(bf16)
        attended = dot_tn(rounded, values).astype(bf16)
        att_ref[rows, cols] = jnp.concatenate(
            [attended[hh * LEN : (hh + 1) * LEN, :] for hh in range(SHARED)], axis=1
        )
        grad_values = dot_nn(rounded, grads)
        grad_dot = dot_nt(values, grads)
        delta = jnp.sum(weights * grad_dot, axis=0, keepdims=True)
        grad_scores = (weights * (grad_dot - delta) * scale).astype(bf16)
        gained = dot_nn(grad_scores, queries) * kg_ref[...]
        mean = jnp.mean(keys * gained, axis=-1, keepdims=True)
        grad_keys = inv * (gained - keys * inv * inv * mean)
        result = jnp.concatenate([grad_keys, grad_values], axis=1).astype(bf16)
        gkv[pl.ds(s * CAP, CAP), :, pl.ds(at, 2 * HEAD)] = result.reshape(CAP, BLK, 2 * HEAD)

    def attend(h):
        wait_all(got2[h], recv_sem.at[1, h])

        def body(step, carry):
            gi, s = step // (CAP // 2), lax.rem(step, CAP // 2) * 2
            one(h, gi, s)
            one(h, gi, s + 1)
            return carry

        lax.fori_loop(0, PER * CAP // 2, body, 0)

        def pack(cb, carry):
            block = gkv[tab_ref[5, cb] & 15]
            out3[h][pl.ds(2 * cb, 2)] = block.reshape(2, BLK // 2, WIDE)
            return carry

        lax.fori_loop(0, 2 * PAIRS, pack, 0)
        exchange(out3[h], got3[h], q, send_sem.at[2, h], recv_sem.at[2, h])

    for h in range(PIECES):
        relay(h, got1, out2, 2, got2, 1)
    for h in range(PIECES):
        attend(h)
        if h > 0:
            relay(h - 1, got3, out4, 3, got4, 3)
    relay(PIECES - 1, got3, out4, 3, got4, 3)
    for h in range(PIECES):
        wait_all(got4[h], recv_sem.at[3, h])
        for j in range(PAIRS):
            color = tab_ref[1, j] & 3
            block = got4[h][pl.ds(4 * color, 4)].reshape(2, BLK, WIDE)
            for gi in range(PER):
                at = (h * PER + gi) * HEAD
                kvg_ref[2 * j : 2 * j + 2, :, at : at + HEAD] = block[
                    :, :, gi * 2 * HEAD : gi * 2 * HEAD + HEAD
                ]
                kvg_ref[2 * j : 2 * j + 2, :, half + at : half + at + HEAD] = block[
                    :, :, gi * 2 * HEAD + HEAD : (gi + 1) * 2 * HEAD
                ]

    for phase in range(4):
        for h in range(PIECES):
            wait_all(got1[h], send_sem.at[phase, h])
    wait_all(every, dest_sem.at[0])
    for which, start in ((0, other), (1, m)):
        done(weight.at[own_rows, columns(start * COLS, COLS)], own_sem.at[0, which])
    done(kv_there, kv_sem.at[0])
    done(out_parts.at[m], om_sem.at[0])
    for k in range(ARRIVALS):
        done(piece(k, pos), z_send.at[k])
        done(out_parts.at[m, e], o_send.at[k])
        for way in range(4):
            done(piece(k, pos) if way < 2 else part(k, pos, 0), r_send.at[k, way])
        done(weight.at[plane_rows(e), columns(0, COLS)], m_send.at[k])


VMEM = pl.BlockSpec(memory_space=pltpu.VMEM)
SMEM = pl.BlockSpec(memory_space=pltpu.SMEM)
HBM = pl.BlockSpec(memory_space=pltpu.HBM)
LIMIT = 62 * 1024 * 1024


def local(
    images,
    vit_gain,
    vit_qkv,
    vit_out,
    kv_weight,
    queries,
    q_gain,
    k_gain,
    out_grad,
    block_image,
    block_dest,
    key_image,
    text_seen,
):
    enc_blocks, block_len, vis = images.shape
    tokens = enc_blocks * block_len
    buffers = [pltpu.VMEM((PEERS, BLK // 2, WIDE), bf16)] * PIECES
    dma = pltpu.SemaphoreType.DMA
    return pl.pallas_call(
        kernel,
        out_shape=(
            jax.ShapeDtypeStruct(queries.shape, bf16),
            jax.ShapeDtypeStruct((enc_blocks, block_len, 2 * KVHEADS * HEAD), bf16),
        ),
        in_specs=[SMEM] * 3 + [VMEM] * 4 + [HBM] * 6,
        out_specs=(VMEM, VMEM),
        scratch_shapes=[
            pltpu.VMEM((tokens, vis), bf16),
            pltpu.VMEM(vit_out.shape, bf16),
            pltpu.VMEM(queries.shape, bf16),
            pltpu.VMEM(queries.shape, bf16),
            pltpu.VMEM((8, 128), jnp.int32),
            pltpu.VMEM((PEERS, 8, 128), jnp.int32),
            pltpu.VMEM((8, 128), jnp.int32),
            pltpu.SMEM((8, 128), jnp.int32),
            pltpu.VMEM((8, SHARED * LEN), jnp.int32),
            pltpu.VMEM((vis, 2 * COLS), bf16),
            pltpu.VMEM((2, PLANES, 48, vis), bf16),
            pltpu.VMEM((VHEADS * VHEAD, vis), bf16),
            pltpu.VMEM((vis, 2 * KVHEADS * HEAD), bf16),
            pltpu.VMEM((PLANES, tokens, ROWS), bf16),
            pltpu.VMEM((tokens, 3 * VHEADS * VHEAD), f32),
            pltpu.VMEM((tokens, 3 * VHEADS * VHEAD), bf16),
            pltpu.VMEM((tokens, VHEADS * VHEAD), bf16),
            pltpu.VMEM((PAIRS, 2 * BLK, vis), bf16),
            buffers,
            pltpu.VMEM((KVHEADS, CAP, SHARED * LEN, HEAD), bf16),
            pltpu.VMEM((CAP * CAP, BLK, WIDE), bf16),
        ]
        + [buffers] * 7
        + [dma((7,)), dma((2,)), dma((2, 2)), dma((2,))]
        + [dma((ARRIVALS,))] * 4
        + [dma((ARRIVALS, 4))] * 2
        + [dma((ARRIVALS,))] * 2
        + [dma((2,))]
        + [dma((4, PIECES))] * 2,
        compiler_params=pltpu.CompilerParams(
            collective_id=0, has_side_effects=True, vmem_limit_bytes=LIMIT
        ),
    )(
        block_image,
        block_dest,
        key_image,
        text_seen.reshape(1, -1),
        vit_gain.reshape(-1, 128),
        q_gain.reshape(1, HEAD),
        k_gain.reshape(1, HEAD),
        images.reshape(tokens, vis),
        vit_qkv,
        vit_out,
        kv_weight,
        queries,
        out_grad,
    )


def solution(mesh):
    everywhere = ("enc", "seq", "mp")
    placed = (
        P(everywhere, None, None),
        P(),
        P(("enc", "mp"), None),
        P(("enc", "mp"), None),
        P("mp", None),
        P(everywhere, None),
        P(),
        P(),
        P(everywhere, None),
        P(everywhere),
        P(everywhere),
        P(everywhere, None),
        P(everywhere),
    )
    return jax.shard_map(
        local,
        mesh=mesh,
        in_specs=placed,
        out_specs=(P(everywhere, None), P(everywhere, None, None)),
        check_vma=False,
    )
```

time: 122 us -> 106 us (0.87)
  Pallas kernels: 110 us -> 101 us
  local copies, waits for them, and re-layouts: 9.35 us -> 3.35 us
    pallas_call x2 -> x1, Pallas kernels: 110 us -> 101 us  [local(): pl.pallas_call(kernel, out_shape=(jax.ShapeDtypeStruct(queries.shape, bf1...]
    unnamed x22 -> x4, local copies, waits for them, and re-layouts: 7.11 us -> 3.35 us
where the time goes in v2:
time: 106 us; the launch traced here: 105 us
  Pallas kernels  101 us (95%)
  local copies, waits for them, and re-layouts  3.35 us (3%)
    pallas_call x1, Pallas kernels, local(): pl.pallas_call(kernel, out_shape=(jax.ShapeDtypeStruct(queries.shape, bf1...  101 us
    unnamed x4, local copies, waits for them, and re-layouts  3.35 us

profile of v2, /device:TPU:32, one launch (start us, length us, event | category | flops | bytes accessed | tf_op | source)
XLA Modules:
  0.0 104.6 jit_solution(10549485366888267342)
XLA Ops:
  0.6 100.6 %shard_map.140 = (bf16[128,4096]{1,0:T(8,128)(2,1)}, bf16[8,64,1024]{2,1,0:T(8,128)(2,1)}) custom-call(s32[8]{0:T(128)} %image_ref.1, s32[8]{0:T(128)} %dest_ref.1, s32[4,4]{1,0:T(4,128)} %kimg_ref.1, s32[1,128]{1,0:T(1,128)} %bitcast.7, f32[10,128]{1,0:T(8,128)} %bitcast.6, f32[1,128]{1,0:T(1,128)} %bitcast.8, f32[1,128]{1,0:T(1,128)} %bitcast.9, ...), custom_call_target="tpu_custom_call" | custom-call | tf_op jit(solution)/shard_map/pallas_call | solution.py:659
  101.2 0.0 copy-start
  101.2 2.4 %copy.17 = bf16[128,4096]{1,0:T(8,128)(2,1)} copy(bf16[128,4096]{1,0:T(8,128)(2,1)} %get-tuple-element.4) | data formatting | bytes 2097152
  103.6 0.0 copy-done
  103.6 1.0 copy.18
Async XLA Ops:
  101.2 2.4 %copy-start = (bf16[8,64,1024]{2,1,0:T(8,128)(2,1)S(1)}, bf16[8,64,1024]{2,1,0:T(8,128)(2,1)}, u32[]{:S(2)}) copy-start(bf16[8,64,1024]{2,1,0:T(8,128)(2,1)} %get-tuple-element.5) | copy-start | bytes 3145732

commit v3 on v2

v3 whole, which is shorter than its diff:
```python
import math

import jax
import jax.numpy as jnp
from jax import lax
from jax.experimental import pallas as pl
from jax.experimental.pallas import tpu as pltpu
from jax.sharding import PartitionSpec as P

VHEADS = 8
VHEAD = 80
HEAD = 128
KVHEADS = 4
SHARED = 8
BLK = 64
LEN = 32
CAP = 4
PEERS = 16
PAIRS = 4
PIECES = 4
PER = KVHEADS // PIECES
WIDE = PER * 2 * HEAD
GROUPS = 2
GROUP = KVHEADS // GROUPS
GWIDE = GROUP * 2 * HEAD
EPS = 1e-05
MESH = pl.DeviceIdType.MESH
f32 = jnp.float32
bf16 = jnp.bfloat16


def dot_nn(left, right):
    return jnp.dot(left, right, preferred_element_type=f32)


def dot_nt(left, right):
    return lax.dot_general(left, right, (((1,), (1,)), ((), ())), preferred_element_type=f32)


def dot_tn(left, right):
    return lax.dot_general(left, right, (((0,), (0,)), ((), ())), preferred_element_type=f32)


def exchange(source, target, me, send_sem, recv_sem, own_sem=None):
    def body(step, carry):
        peer = lax.rem(me + step, PEERS)
        pltpu.make_async_remote_copy(
            src_ref=source.at[peer],
            dst_ref=target.at[me],
            send_sem=send_sem,
            recv_sem=recv_sem,
            device_id={"seq": peer},
            device_id_type=MESH,
        ).start()
        return carry

    lax.fori_loop(1, PEERS, body, 0)
    if own_sem is None:
        target[me] = source[me]
    else:
        pltpu.make_async_copy(source.at[me], target.at[me], own_sem).start()


def wait_all(buffer, sem):
    view = buffer.at[pl.ds(0, PEERS - 1)]
    pltpu.make_async_copy(view, view, sem).wait()


def split_colors(src_partner, dst_partner, doublings):
    n = src_partner.shape[0]
    row = lax.broadcasted_iota(jnp.int32, (n, n), 0)
    col = lax.broadcasted_iota(jnp.int32, (n, n), 1)
    src_b = jnp.where(src_partner, 1.0, 0.0).astype(bf16)
    dst_b = jnp.where(dst_partner, 1.0, 0.0).astype(bf16)
    power = dot_nn(src_b, dst_b).astype(bf16)
    total = jnp.where(row == col, 1.0, 0.0) + power.astype(f32)
    yield
    for _ in range(doublings - 1):
        power = dot_nn(power, power).astype(bf16)
        total = total + dot_nn(total.astype(bf16), power)
        yield
    orbit = total > 0.5
    lead_c = jnp.min(jnp.where(orbit, col, n), axis=1, keepdims=True)
    lead_r = jnp.min(jnp.where(orbit, row, n), axis=0, keepdims=True)
    other_c = jnp.sum(jnp.where(src_partner, lead_r, 0), axis=1, keepdims=True)
    other_r = jnp.sum(jnp.where(src_partner, lead_c, 0), axis=0, keepdims=True)
    return (lead_c < other_c).astype(jnp.int32), (lead_r < other_r).astype(jnp.int32)


def color_tables(dest, me):
    n = dest.shape[0]
    row = lax.broadcasted_iota(jnp.int32, (n, n), 0)
    col = lax.broadcasted_iota(jnp.int32, (n, n), 1)
    dest_t = jnp.transpose(dest.astype(f32)).astype(jnp.int32)
    owner_c, owner_r = dest >> 4, dest_t >> 4
    parity_same = (row & 1) == (col & 1)
    src_same = ((row >> 3) == (col >> 3)) & parity_same
    dst_same = (owner_c == owner_r) & parity_same
    rank_c = jnp.sum(jnp.where(dst_same & (col < row), 1, 0), axis=1, keepdims=True)
    rank_r = jnp.sum(jnp.where(dst_same & (row < col), 1, 0), axis=0, keepdims=True)
    src_partner = col == (row ^ 2)
    dst_partner = dst_same & (rank_r == (rank_c ^ 1))
    yield
    one_c, one_r = yield from split_colors(src_partner, dst_partner, 5)
    yield
    alike = (one_c == one_r) & (row != col)
    two_c, _ = yield from split_colors(src_same & alike, dst_same & alike, 4)
    yield
    color = jnp.broadcast_to(2 * one_c + two_c, (n, n))
    src = row >> 3
    pair = (row & 7) >> 1
    half = row & 1
    even = half == 0
    mine = src == me
    turn, turn2 = me // 4, me // 8

    def pick(mask, value):
        return jnp.sum(jnp.where(mask, value, 0), axis=0, keepdims=True)

    rows = [
        pick(mine & even & (color == col), pair),
        pick(mine & even & (pair == col), color),
        pick(even & (color == turn2) & (owner_c == col), src),
        pick(even & (color == turn) & (src == col), owner_c),
        pick((owner_c == me) & ((dest & 15) == col), 2 * color + half + 1) - 1,
        pick((owner_c == me) & (2 * color + half == col), dest & 15),
        pick(even & (color == 2 + turn2) & (owner_c == col), src),
    ]
    rows += [jnp.zeros_like(rows[0])]
    return jnp.concatenate(rows, axis=0)


PLANES = 8
ROWS = 160
PIECE = 256
ARRIVALS = PLANES - 1
WINDOW = 384
LOG2E = 1.4426950408889634


def softmax_over_rows(scores, allowed, scale):
    masked = jnp.where(allowed, scores, -jnp.inf)
    top = jnp.max(masked, axis=0, keepdims=True)
    terms = jnp.exp2((masked - top) * (scale * LOG2E))
    return terms * (1.0 / jnp.sum(terms, axis=0, keepdims=True))


def kernel(
    image_ref,
    dest_ref,
    kimg_ref,
    seen_ref,
    gain_ref,
    qg_ref,
    kg_ref,
    x_hbm,
    qkv_hbm,
    out_hbm,
    kv_hbm,
    q_hbm,
    og_hbm,
    att_hbm,
    back_hbm,
    tab_hbm,
    x_ref,
    own_out,
    own_qkv,
    q_ref,
    og_ref,
    att_ref,
    dest_tile,
    every,
    tab_tile,
    tab_ref,
    seen_rows,
    weight,
    out_parts,
    out_ref,
    kv_ref,
    normed,
    summed,
    mixed,
    att,
    hidden,
    pay,
    qn,
    gkv,
    got1,
    out2,
    got2,
    out3,
    got3,
    out4,
    local_sem,
    dest_sem,
    own_sem,
    kv_sem,
    z_send,
    z_recv,
    o_send,
    o_recv,
    r_send,
    r_recv,
    m_send,
    m_recv,
    ro_send,
    ro_recv,
    mo_send,
    mo_recv,
    oo_sem,
    att_sem,
    own_back,
    f_send,
    f_recv,
    send_sem,
    recv_sem,
):
    pairs_here, span, vis = x_ref.shape
    tokens = pairs_here * span
    e, q, m = lax.axis_index("enc"), lax.axis_index("seq"), lax.axis_index("mp")
    other = 1 - m
    d = 1 - 2 * m
    stride = 1 + 3 * m
    pos = lax.rem(q // stride, 4)
    ring = q - pos * stride
    left, right, far = lax.rem(pos + 3, 4), lax.rem(pos + 1, 4), lax.rem(pos + 2, 4)
    ahead, behind = lax.rem(e + d + PLANES, PLANES), lax.rem(e - d + PLANES, PLANES)
    to_left, to_right = {"seq": ring + left * stride}, {"seq": ring + right * stride}
    to_ahead, to_behind, to_mate = {"enc": ahead}, {"enc": behind}, {"mp": other}

    def remote(source, target, send, recv, device):
        pltpu.make_async_remote_copy(
            src_ref=source,
            dst_ref=target,
            send_sem=send,
            recv_sem=recv,
            device_id=device,
            device_id_type=MESH,
        ).start()

    def done(view, sem):
        pltpu.make_async_copy(view, view, sem).wait()

    half_rows = ROWS // 2
    own_rows = pl.ds(pl.multiple_of(m * half_rows, half_rows), half_rows)
    mate_rows = pl.ds(pl.multiple_of(other * half_rows, half_rows), half_rows)
    kv_half = kv_hbm.shape[0]
    kv_rows = pl.ds(pl.multiple_of(m * kv_half, kv_half), kv_half)
    copies = [
        pltpu.make_async_copy(source, target, local_sem.at[index])
        for index, (source, target) in enumerate(
            (
                (qkv_hbm, own_qkv),
                (x_hbm, x_ref),
                (out_hbm, own_out),
                (kv_hbm, kv_ref.at[kv_rows]),
                (q_hbm, q_ref),
                (og_hbm, og_ref),
                (tab_tile, tab_ref),
                (tab_tile, tab_hbm),
            )
        )
    ]
    qkv_copy, x_copy, out_copy, kv_copy, q_copy, og_copy, tab_copy, tab_out = copies
    for copy in copies[:-2]:
        copy.start()

    barrier = pltpu.get_barrier_semaphore()

    def hello(step, carry):
        pl.semaphore_signal(
            barrier, inc=1, device_id={"seq": lax.rem(q + step, PEERS)}, device_id_type=MESH
        )
        return carry

    lax.fori_loop(1, PEERS, hello, 0)
    for device in (to_ahead, to_behind, to_mate):
        pl.semaphore_signal(barrier, inc=1, device_id=device, device_id_type=MESH)

    sub = lax.broadcasted_iota(jnp.int32, (8, 128), 0)
    lane = lax.broadcasted_iota(jnp.int32, (8, 128), 1)
    tile = jnp.zeros((8, 128), jnp.int32)
    for block in range(8):
        tile = jnp.where(sub == block, dest_ref[block], tile)
    dest_tile[...] = tile
    every[q] = tile
    spread = jnp.where(lane // LEN == sub, seen_ref[...].astype(f32), 0.0).astype(bf16)
    wide = (128, SHARED * LEN)
    place = lax.rem(lax.broadcasted_iota(jnp.int32, wide, 0), LEN) == lax.rem(
        lax.broadcasted_iota(jnp.int32, wide, 1), LEN
    )
    seen_rows[...] = dot_nn(spread, jnp.where(place, 1.0, 0.0).astype(bf16)).astype(jnp.int32)
    gain = jnp.concatenate([gain_ref[t : t + 1, :] for t in range(vis // 128)], axis=1)
    out_copy.wait()
    have = own_out.shape[0]
    for place in range(4):
        at = min(place * WINDOW, vis - WINDOW)
        out_parts[m, e, place, 0:have, :] = own_out[:, at : at + WINDOW]
    qkv_copy.wait()
    for p in range(8):
        count = min(PIECE, own_qkv.shape[1] - p * PIECE)
        weight[p, e, own_rows, 0:count] = own_qkv[:, p * PIECE : p * PIECE + count]
    pl.semaphore_wait(barrier, PEERS + 2)

    mine = 4 * m + pos

    def side(core):
        return pl.ds(4 * core, 4)

    for which, core in ((0, other), (1, m)):
        view = weight.at[side(core), e, own_rows]
        remote(view, view, own_sem.at[0, which], own_sem.at[1, which], to_mate)

    def send_z(plane, which, arrival):
        view = weight.at[mine, plane, mate_rows if which else own_rows]
        device = to_behind if arrival % 2 else to_ahead
        remote(view, view, z_send.at[arrival, which], z_recv.at[arrival, which], device)

    send_z(e, 0, 0)
    send_z(e, 0, 1)
    view = out_parts.at[m, e]
    remote(view, view, oo_sem.at[0], oo_sem.at[1], to_mate)

    def send_dest(step, carry):
        peer = lax.rem(q + step, PEERS)
        remote(dest_tile, every.at[q], dest_sem.at[0], dest_sem.at[1], {"seq": peer})
        return carry

    lax.fori_loop(1, PEERS, send_dest, 0)
    done(weight.at[side(m), e, mate_rows], own_sem.at[1, 0])
    send_z(e, 1, 0)
    send_z(e, 1, 1)
    kv_there = kv_ref.at[kv_rows]

    def send_out(plane, arrival):
        view = out_parts.at[m, plane, pos]
        device = to_behind if arrival % 2 else to_ahead
        remote(view, view, o_send.at[arrival], o_recv.at[arrival], device)

    def plane_of(arrival):
        hops = arrival // 2 + 1
        if arrival % 2 == 0:
            return lax.rem(e - d * hops + PLANES, PLANES)
        return lax.rem(e + d * hops + PLANES, PLANES)

    def piece(k, place):
        return weight.at[4 * m + place, plane_of(k)]

    def part(k, place, which):
        return weight.at[4 * m + place, plane_of(k), pl.ds(which * half_rows, half_rows)]

    width = VHEADS * VHEAD

    def norm_jobs():
        x_copy.wait()
        for t in range(tokens // 64):
            rows = slice(t * 64, t * 64 + 64)
            values = x_ref[t // 2, t % 2 * 64 : t % 2 * 64 + 64, :].astype(f32)
            center = values - jnp.mean(values, axis=-1, keepdims=True)
            spread = jnp.mean(center * center, axis=-1, keepdims=True)
            result = (center * lax.rsqrt(spread + EPS) * gain).astype(bf16)
            for plane in range(PLANES):
                normed[plane, rows, :] = result[:, plane * ROWS : (plane + 1) * ROWS]
            yield

    def table_jobs():
        wait_all(every, dest_sem.at[1])
        tab_tile[...] = yield from color_tables(every[...].reshape(PEERS * 8, 128), q)
        tab_copy.start()
        tab_out.start()

    def add_plane(plane, mode, p):
        count = min(PIECE, 3 * width - p * PIECE)
        cols = slice(p * PIECE, p * PIECE + count)
        found = dot_nn(normed[plane], weight[p, plane, :, 0:count])
        if mode == 0:
            summed[:, cols] = found
        elif mode == 1:
            summed[:, cols] += found
        else:
            total = (summed[:, cols] + found).astype(bf16)
            mixed[:, :, cols] = total.reshape(PAIRS, span, count)

    def plane_jobs(k):
        if k < 0:
            done(weight.at[side(other), e, mate_rows], own_sem.at[1, 1])
            plane = e
        else:
            same = k ^ 1 if k < ARRIVALS - 1 else k
            done(weight.at[side(m), e], m_recv.at[same])
            plane = plane_of(k)
        mode = 0 if k < 0 else 1 if k < ARRIVALS - 1 else 2
        for p in range(8):
            add_plane(plane, mode, p)
            if p % 3 == 2:
                yield
        yield

    def out_jobs(k):
        if k < 0:
            plane = e
            done(out_parts.at[m, e], oo_sem.at[1])
        else:
            plane = plane_of(k)
            done(out_parts.at[m, e], mo_recv.at[k ^ 1 if k < ARRIVALS - 1 else k])
        both = []
        for core in range(2):
            parts = [out_parts[core, plane, place, 0:have, :] for place in range(4)]
            parts[3] = parts[3][:, 4 * WINDOW - vis :]
            both.append(jnp.concatenate(parts, axis=1).astype(f32))
        rows = pl.ds(pl.multiple_of(2 * have * plane, 2 * have), 2 * have)
        out_ref[rows, :] = jnp.concatenate(both, axis=0).astype(bf16)
        yield

    queue = [norm_jobs(), table_jobs(), plane_jobs(-1)]

    def pump(steps):
        while queue and steps > 0:
            try:
                next(queue[0])
                steps -= 1
            except StopIteration:
                queue.pop(0)

    send_out(e, 0)
    send_out(e, 1)
    remote(kv_hbm, kv_there, kv_sem.at[0], kv_sem.at[1], to_mate)
    pump(2)
    hops = ((0, 1), (2, 3), (4, 5), (6,))
    for t in range(len(hops) + 2):
        if t < len(hops):
            for which in range(2):
                for k in hops[t]:
                    rows = mate_rows if which else own_rows
                    done(weight.at[mine, plane_of(k), rows], z_recv.at[k, which])
                    if k + 2 < ARRIVALS:
                        send_z(plane_of(k), which, k + 2)
            for k in hops[t]:
                view = piece(k, pos)
                remote(view, view, r_send.at[k, 0], r_recv.at[k, 0], to_right)
                remote(view, view, r_send.at[k, 1], r_recv.at[k, 1], to_left)
            for k in hops[t]:
                view = out_parts.at[m, plane_of(k), pos]
                done(view, o_recv.at[k])
                if k + 2 < ARRIVALS:
                    send_out(plane_of(k), k + 2)
                remote(view, view, ro_send.at[k, 0], ro_recv.at[k, 0], to_right)
                remote(view, view, ro_send.at[k, 1], ro_recv.at[k, 1], to_left)
        pump(2)
        if 0 <= t - 1 < len(hops):
            for k in hops[t - 1]:
                view = part(k, left, 0)
                done(piece(k, left), r_recv.at[k, 0])
                remote(view, view, r_send.at[k, 2], r_recv.at[k, 2], to_right)
                view = part(k, right, 1)
                done(piece(k, right), r_recv.at[k, 1])
                remote(view, view, r_send.at[k, 3], r_recv.at[k, 3], to_left)
            for k in hops[t - 1]:
                from_left = out_parts.at[m, plane_of(k), left]
                from_right = out_parts.at[m, plane_of(k), right]
                done(from_left, ro_recv.at[k, 0])
                done(from_right, ro_recv.at[k, 1])
                if k % 2 == 0:
                    remote(from_left, from_left, ro_send.at[k, 2], ro_recv.at[k, 2], to_right)
                else:
                    remote(from_right, from_right, ro_send.at[k, 2], ro_recv.at[k, 2], to_left)
        pump(2)
        if 0 <= t - 2 < len(hops):
            for k in hops[t - 2]:
                done(part(k, far, 0), r_recv.at[k, 2])
                done(part(k, far, 1), r_recv.at[k, 3])
                view = weight.at[side(m), plane_of(k)]
                remote(view, view, m_send.at[k], m_recv.at[k], to_mate)
            for k in hops[t - 2]:
                done(out_parts.at[m, plane_of(k), far], ro_recv.at[k, 2])
                view = out_parts.at[m, plane_of(k)]
                remote(view, view, mo_send.at[k], mo_recv.at[k], to_mate)
        pump(2)
        if t == 1:
            queue.append(out_jobs(-1))
        if 0 <= t - 2 < len(hops):
            queue.extend(plane_jobs(k) for k in hops[t - 2])
        if 0 <= t - 3 < len(hops):
            queue.extend(out_jobs(k) for k in hops[t - 3])
    pump(1000)
    queue.append(out_jobs(ARRIVALS - 1))

    row = lax.broadcasted_iota(jnp.int32, (span, span), 0)
    col = lax.broadcasted_iota(jnp.int32, (span, span), 1)
    near = (row // BLK) == (col // BLK)

    def window(head):
        first, last = head * VHEAD // 128, ((head + 1) * VHEAD - 1) // 128
        return first, last, first * 128, (last - first + 1) * 128

    def attend_pair(c):
        pair = tab_ref[0, c] & 3
        allowed = near | (image_ref[2 * pair] == image_ref[2 * pair + 1])
        insides, scores = [], []
        for head in range(VHEADS):
            _, _, base, cut = window(head)
            lanes = lax.broadcasted_iota(jnp.int32, (span, cut), 1) + base
            inside = (lanes >= head * VHEAD) & (lanes < (head + 1) * VHEAD)
            query = jnp.where(inside, mixed[pair, :, base : base + cut], jnp.zeros((), bf16))
            key = mixed[pair, :, width + base : width + base + cut]
            insides.append(inside)
            scores.append(dot_nt(key, query))
        weights = [
            softmax_over_rows(found, allowed, 1.0 / math.sqrt(VHEAD)).astype(bf16)
            for found in scores
        ]
        tiles = [None] * (width // 128)
        for head in range(VHEADS):
            first, last, base, cut = window(head)
            value = mixed[pair, :, 2 * width + base : 2 * width + base + cut]
            result = dot_tn(weights[head], value)
            for t in range(first, last + 1):
                at = (t - first) * 128
                found = result[:, at : at + 128]
                if tiles[t] is not None:
                    found = jnp.where(insides[head][:, at : at + 128], found, tiles[t])
                tiles[t] = found
        att[c] = jnp.concatenate(tiles, axis=1).astype(bf16)

    half = KVHEADS * HEAD
    tab_copy.wait()
    for a in range(2):
        pairs = (2 * a, 2 * a + 1)

        def attend_pairs(c, carry):
            attend_pair(c)
            return carry

        lax.fori_loop(pairs[0], pairs[1] + 1, attend_pairs, 0)
        if a == 0:
            pump(1000)
        attended = jnp.concatenate([att[c] for c in pairs], axis=0)

        def project(t, carry):
            cols = pl.ds(pl.multiple_of(t * 256, 256), 256)
            tokens_in = jnp.concatenate(
                [x_ref[tab_ref[0, c] & 3, :, cols] for c in pairs], axis=0
            )
            total = tokens_in.astype(f32) + dot_nn(attended, out_ref[:, cols])
            hidden[a, :, cols] = total.astype(bf16)
            return carry

        lax.fori_loop(0, vis // 256, project, 0)
        if a == 0:
            kv_copy.wait()
            done(kv_there, kv_sem.at[1])
        for b in range(GROUPS):
            for t in range(GROUP):
                at = (b * GROUP + t) * HEAD
                both = jnp.concatenate(
                    [kv_ref[:, at : at + HEAD], kv_ref[:, half + at : half + at + HEAD]], axis=1
                )
                pay[a][b][:, :, t * 2 * HEAD : (t + 1) * 2 * HEAD] = (
                    dot_nn(hidden[a], both).astype(bf16).reshape(PEERS, BLK // 4, 2 * HEAD)
                )
            exchange(pay[a][b], got1[a][b], q, f_send.at[0, a, b], f_recv.at[0, a, b])

    q_copy.wait()

    def norm_queries(g, carry):
        block = q_ref[:, pl.ds(pl.multiple_of(g * SHARED * HEAD, HEAD), SHARED * HEAD)]
        for hh in range(SHARED):
            x = block[:, hh * HEAD : (hh + 1) * HEAD].astype(f32)
            inv = lax.rsqrt(jnp.mean(x * x, axis=-1, keepdims=True) + EPS)
            y = (x * inv * qg_ref[...]).astype(bf16)
            for s in range(CAP):
                qn[g, s, hh * LEN : (hh + 1) * LEN, :] = y[s * LEN : (s + 1) * LEN, :]
        return carry

    lax.fori_loop(0, KVHEADS, norm_queries, 0)
    og_copy.wait()

    def shuffle(got, out, table):
        def body(index, carry):
            out[index] = got[tab_ref[table, index] & 15]
            return carry

        lax.fori_loop(0, PEERS, body, 0)

    def relay(a, b):
        wait_all(got1[a][b], f_recv.at[0, a, b])
        shuffle(got1[a][b], out2[a][b], 6 if a else 2)
        exchange(out2[a][b], got2[b].at[pl.ds(a * PEERS, PEERS)], q, f_send.at[1, a, b], f_recv.at[1, a, b])

    def give_back(h):
        wait_all(got3[h], recv_sem.at[0, h])
        shuffle(got3[h], out4[h], 3)
        exchange(out4[h], back_hbm.at[h], q, send_sem.at[1, h], recv_sem.at[1, h], own_back.at[h])

    def one(h, gi, s):
        g = h * PER + gi
        at = pl.multiple_of(gi * 2 * HEAD, 2 * HEAD)
        group = h * PER // GROUP
        from_col = pl.multiple_of((h * PER % GROUP + gi) * 2 * HEAD, 2 * HEAD)
        blocks, masks = [], []
        seen = seen_rows[pl.ds(s, 1), :]
        for kb in range(CAP):
            index = tab_ref[4, s * CAP + kb]
            start = 4 * (jnp.maximum(index, 0) & 7)
            block = got2[group][pl.ds(start, 4), :, pl.ds(from_col, 2 * HEAD)]
            blocks.append(
                jnp.where(index >= 0, block, jnp.zeros((), bf16)).reshape(BLK, 2 * HEAD)
            )
            masks.append(jnp.broadcast_to(kimg_ref[s, kb] < seen, (BLK, SHARED * LEN)))
        keyval = jnp.concatenate(blocks, axis=0)
        allowed = jnp.concatenate(masks, axis=0)
        keys = keyval[:, :HEAD].astype(f32)
        values = keyval[:, HEAD:]
        inv = lax.rsqrt(jnp.mean(keys * keys, axis=-1, keepdims=True) + EPS)
        kn = (keys * inv * kg_ref[...]).astype(bf16)
        queries = qn[g, s]
        rows = pl.ds(pl.multiple_of(s * LEN, LEN), LEN)
        cols = pl.ds(pl.multiple_of(g * SHARED * HEAD, SHARED * HEAD), SHARED * HEAD)
        grad_row = og_ref[rows, cols]
        grads = jnp.concatenate(
            [grad_row[:, hh * HEAD : (hh + 1) * HEAD] for hh in range(SHARED)], axis=0
        )
        scale = 1.0 / math.sqrt(HEAD)
        weights = softmax_over_rows(dot_nt(kn, queries), allowed, scale)
        rounded = weights.astype(bf16)
        attended = dot_tn(rounded, values).astype(bf16)
        att_ref[rows, cols] = jnp.concatenate(
            [attended[hh * LEN : (hh + 1) * LEN, :] for hh in range(SHARED)], axis=1
        )
        grad_values = dot_nn(rounded, grads)
        grad_dot = dot_nt(values, grads)
        delta = jnp.sum(weights * grad_dot, axis=0, keepdims=True)
        grad_scores = (weights * (grad_dot - delta) * scale).astype(bf16)
        gained = dot_nn(grad_scores, queries) * kg_ref[...]
        mean = jnp.mean(keys * gained, axis=-1, keepdims=True)
        grad_keys = inv * (gained - keys * inv * inv * mean)
        result = jnp.concatenate([grad_keys, grad_values], axis=1).astype(bf16)
        gkv[pl.ds(s * CAP, CAP), :, pl.ds(at, 2 * HEAD)] = result.reshape(CAP, BLK, 2 * HEAD)

    def attend(h):
        if h * PER % GROUP == 0:
            for a in range(2):
                wait_all(got2[h * PER // GROUP], f_recv.at[1, a, h * PER // GROUP])

        def body(step, carry):
            gi, s = step // (CAP // 2), lax.rem(step, CAP // 2) * 2
            one(h, gi, s)
            one(h, gi, s + 1)
            return carry

        lax.fori_loop(0, PER * CAP // 2, body, 0)

        def pack(cb, carry):
            block = gkv[tab_ref[5, cb] & 15]
            out3[h][pl.ds(2 * cb, 2)] = block.reshape(2, BLK // 2, WIDE)
            return carry

        lax.fori_loop(0, 2 * PAIRS, pack, 0)
        exchange(out3[h], got3[h], q, send_sem.at[0, h], recv_sem.at[0, h])
        cols = slice(h * PER * SHARED * HEAD, (h + 1) * PER * SHARED * HEAD)
        pltpu.make_async_copy(att_ref.at[:, cols], att_hbm.at[:, cols], att_sem.at[h]).start()

    for a in range(2):
        for b in range(GROUPS):
            relay(a, b)
    for h in range(PIECES):
        attend(h)
        if h > 0:
            give_back(h - 1)
    give_back(PIECES - 1)
    for h in range(PIECES):
        wait_all(back_hbm.at[h], recv_sem.at[1, h])

    tab_out.wait()
    for h in range(PIECES):
        cols = slice(h * PER * SHARED * HEAD, (h + 1) * PER * SHARED * HEAD)
        pltpu.make_async_copy(att_ref.at[:, cols], att_hbm.at[:, cols], att_sem.at[h]).wait()
        pltpu.make_async_copy(out4[h].at[q], back_hbm.at[h, q], own_back.at[h]).wait()
        for phase in range(2):
            wait_all(got3[h], send_sem.at[phase, h])
    for a in range(2):
        for b in range(GROUPS):
            for phase in range(2):
                wait_all(got1[a][b], f_send.at[phase, a, b])
    wait_all(every, dest_sem.at[0])
    for which in range(2):
        done(weight.at[side(m), e, own_rows], own_sem.at[0, which])
    done(kv_there, kv_sem.at[0])
    done(out_parts.at[m, e], oo_sem.at[0])
    for k in range(ARRIVALS):
        for which in range(2):
            done(weight.at[mine, e, own_rows], z_send.at[k, which])
        done(out_parts.at[m, e, pos], o_send.at[k])
        done(out_parts.at[m, e], mo_send.at[k])
        for way in range(3):
            done(out_parts.at[m, e, pos], ro_send.at[k, way])
        for way in range(4):
            done(piece(k, pos) if way < 2 else part(k, pos, 0), r_send.at[k, way])
        done(weight.at[side(m), e], m_send.at[k])


def place_kernel(tab_ref, att_hbm, back_hbm, att_out, kvg_out, att, back, kvg, sems):
    parts = 4
    rows = att.shape[0] // parts
    att_in, back_in, att_back, kvg_back = [], [], [], []
    for t in range(parts):
        view = pl.ds(t * rows, rows)
        att_in.append(pltpu.make_async_copy(att_hbm.at[view], att.at[view], sems.at[0, t]))
        att_back.append(pltpu.make_async_copy(att.at[view], att_out.at[view], sems.at[1, t]))
    for h in range(PIECES):
        back_in.append(pltpu.make_async_copy(back_hbm.at[h], back.at[h], sems.at[2, h]))
    for j in range(PAIRS):
        view = pl.ds(2 * j, 2)
        kvg_back.append(pltpu.make_async_copy(kvg.at[view], kvg_out.at[view], sems.at[3, j]))
    for copy in back_in + att_in:
        copy.start()
    for copy in back_in:
        copy.wait()
    half = KVHEADS * HEAD
    for j in range(PAIRS):
        color = tab_ref[1, j] & 3
        for g in range(KVHEADS):
            at = g % PER * 2 * HEAD
            block = back[g // PER, pl.ds(4 * color, 4), :, at : at + 2 * HEAD]
            block = block.reshape(2, BLK, 2 * HEAD)
            kvg[2 * j : 2 * j + 2, :, g * HEAD : (g + 1) * HEAD] = block[:, :, :HEAD]
            kvg[2 * j : 2 * j + 2, :, half + g * HEAD : half + (g + 1) * HEAD] = block[:, :, HEAD:]
        kvg_back[j].start()
    for coming, going in zip(att_in, att_back):
        coming.wait()
        going.start()
    for copy in kvg_back + att_back:
        copy.wait()


VMEM = pl.BlockSpec(memory_space=pltpu.VMEM)
SMEM = pl.BlockSpec(memory_space=pltpu.SMEM)
HBM = pl.BlockSpec(memory_space=pltpu.HBM)
LIMIT = 62 * 1024 * 1024


def local(
    images,
    vit_gain,
    vit_qkv,
    vit_out,
    kv_weight,
    queries,
    q_gain,
    k_gain,
    out_grad,
    block_image,
    block_dest,
    key_image,
    text_seen,
):
    enc_blocks, block_len, vis = images.shape
    tokens = enc_blocks * block_len
    buffers = [pltpu.VMEM((PEERS, BLK // 2, WIDE), bf16)] * PIECES
    chunks = [[pltpu.VMEM((PEERS, BLK // 4, GWIDE), bf16)] * GROUPS] * 2
    dma = pltpu.SemaphoreType.DMA
    attended, back, tables = pl.pallas_call(
        kernel,
        out_shape=(
            jax.ShapeDtypeStruct(queries.shape, bf16),
            jax.ShapeDtypeStruct((PIECES, PEERS, BLK // 2, WIDE), bf16),
            jax.ShapeDtypeStruct((8, 128), jnp.int32),
        ),
        in_specs=[SMEM] * 3 + [VMEM] * 4 + [HBM] * 6,
        out_specs=(HBM, HBM, HBM),
        scratch_shapes=[
            pltpu.VMEM((PAIRS, 2 * BLK, vis), bf16),
            pltpu.VMEM(vit_out.shape, bf16),
            pltpu.VMEM(vit_qkv.shape, bf16),
            pltpu.VMEM(queries.shape, bf16),
            pltpu.VMEM(queries.shape, bf16),
            pltpu.VMEM(queries.shape, bf16),
            pltpu.VMEM((8, 128), jnp.int32),
            pltpu.VMEM((PEERS, 8, 128), jnp.int32),
            pltpu.VMEM((8, 128), jnp.int32),
            pltpu.SMEM((8, 128), jnp.int32),
            pltpu.VMEM((8, SHARED * LEN), jnp.int32),
            pltpu.VMEM((8, PLANES, ROWS, PIECE), bf16),
            pltpu.VMEM((2, PLANES, 4, 48, WINDOW), bf16),
            pltpu.VMEM((VHEADS * VHEAD, vis), bf16),
            pltpu.VMEM((vis, 2 * KVHEADS * HEAD), bf16),
            pltpu.VMEM((PLANES, tokens, ROWS), bf16),
            pltpu.VMEM((tokens, 3 * VHEADS * VHEAD), f32),
            pltpu.VMEM((PAIRS, 2 * BLK, 3 * VHEADS * VHEAD), bf16),
            pltpu.VMEM((PAIRS, 2 * BLK, VHEADS * VHEAD), bf16),
            pltpu.VMEM((2, 4 * BLK, vis), bf16),
            chunks,
            pltpu.VMEM((KVHEADS, CAP, SHARED * LEN, HEAD), bf16),
            pltpu.VMEM((CAP * CAP, BLK, WIDE), bf16),
            chunks,
            chunks,
            [pltpu.VMEM((2 * PEERS, BLK // 4, GWIDE), bf16)] * GROUPS,
            buffers,
            buffers,
            buffers,
            dma((8,)),
            dma((2,)),
            dma((2, 2)),
            dma((2,)),
        ]
        + [dma((ARRIVALS, 2))] * 2
        + [dma((ARRIVALS,))] * 2
        + [dma((ARRIVALS, 4))] * 2
        + [dma((ARRIVALS,))] * 2
        + [dma((ARRIVALS, 3))] * 2
        + [dma((ARRIVALS,))] * 2
        + [dma((2,)), dma((PIECES,)), dma((PIECES,))]
        + [dma((2, 2, GROUPS))] * 2
        + [dma((2, PIECES))] * 2,
        compiler_params=pltpu.CompilerParams(
            collective_id=0, has_side_effects=True, vmem_limit_bytes=LIMIT
        ),
    )(
        block_image,
        block_dest,
        key_image,
        text_seen.reshape(1, -1),
        vit_gain.reshape(-1, 128),
        q_gain.reshape(1, HEAD),
        k_gain.reshape(1, HEAD),
        images.reshape(PAIRS, 2 * BLK, vis),
        vit_qkv,
        vit_out,
        kv_weight,
        queries,
        out_grad,
    )
    attended, kv_grad = pl.pallas_call(
        place_kernel,
        out_shape=(
            jax.ShapeDtypeStruct(queries.shape, bf16),
            jax.ShapeDtypeStruct((enc_blocks, block_len, 2 * KVHEADS * HEAD), bf16),
        ),
        in_specs=[SMEM, HBM, HBM],
        out_specs=(HBM, HBM),
        scratch_shapes=[
            pltpu.VMEM(queries.shape, bf16),
            pltpu.VMEM((PIECES, PEERS, BLK // 2, WIDE), bf16),
            pltpu.VMEM((enc_blocks, block_len, 2 * KVHEADS * HEAD), bf16),
            dma((4, 4)),
        ],
        compiler_params=pltpu.CompilerParams(vmem_limit_bytes=LIMIT),
    )(tables, attended, back)
    return attended, kv_grad


def solution(mesh):
    everywhere = ("enc", "seq", "mp")
    placed = (
        P(everywhere, None, None),
        P(),
        P(("enc", "mp"), None),
        P(("enc", "mp"), None),
        P("mp", None),
        P(everywhere, None),
        P(),
        P(),
        P(everywhere, None),
        P(everywhere),
        P(everywhere),
        P(everywhere, None),
        P(everywhere),
    )
    return jax.shard_map(
        local,
        mesh=mesh,
        in_specs=placed,
        out_specs=(P(everywhere, None), P(everywhere, None, None)),
        check_vma=False,
    )
```

time: 106 us -> 99.5 us (0.939)
  local copies, waits for them, and re-layouts: 3.35 us -> 0 us
  Pallas kernels: 101 us -> 98 us
    pallas_call x1, Pallas kernels: 101 us -> 94.6 us  [local(): pl.pallas_call(kernel, out_shape=(jax.ShapeDtypeStruct(queries.shape, bf1...]
    pallas_call x0 -> x1, Pallas kernels: none -> 3.4 us  [local(): pl.pallas_call(place_kernel, out_shape=(jax.ShapeDtypeStruct(queries.shap...]
    unnamed x4 -> x0, local copies, waits for them, and re-layouts: 3.35 us -> none
where the time goes in v3:
time: 99.5 us; the launch traced here: 98.8 us
  Pallas kernels  98 us (98%)
    pallas_call x1, Pallas kernels, local(): pl.pallas_call(kernel, out_shape=(jax.ShapeDtypeStruct(queries.shape, bf1...  94.6 us
    pallas_call x1, Pallas kernels, local(): pl.pallas_call(place_kernel, out_shape=(jax.ShapeDtypeStruct(queries.shap...  3.4 us

profile of v3, /device:TPU:32, one launch (start us, length us, event | category | flops | bytes accessed | tf_op | source)
XLA Modules:
  0.0 98.8 jit_solution(8010203477112186302)
XLA Ops:
  0.6 94.6 %shard_map.140 = (bf16[128,4096]{1,0:T(8,128)(2,1)}, bf16[4,16,32,256]{3,2,1,0:T(8,128)(2,1)}, s32[8,128]{1,0:T(8,128)}) custom-call(s32[8]{0:T(128)} %image_ref.1, s32[8]{0:T(128)} %dest_ref.1, s32[4,4]{1,0:T(4,128)} %kimg_ref.1, s32[1,128]{1,0:T(1,128)} %bitcast.7, f32[10,128]{1,0:T(8,128)} %bitcast.6, f32[1,128]{1,0:T(1,128)} %bitcast.8, ...), custom_call_target="tpu_custom_call" | custom-call | tf_op jit(solution)/shard_map/pallas_call | solution.py:762
  95.2 3.4 %shard_map.141 = (bf16[128,4096]{1,0:T(8,128)(2,1)}, bf16[8,64,1024]{2,1,0:T(8,128)(2,1)}) custom-call(s32[8,128]{1,0:T(8,128)} %get-tuple-element.5.tab_ref, bf16[128,4096]{1,0:T(8,128)(2,1)} %get-tuple-element.6.att_hbm, bf16[4,16,32,256]{3,2,1,0:T(8,128)(2,1)} %get-tuple-element.7.back_hbm), custom_call_target="tpu_custom_call" | custom-call | tf_op jit(solution)/shard_map/pallas_call | solution.py:833

commit v4 on v3

--- a/solution.py
+++ b/solution.py
@@ -17,7 +17,7 @@
 CAP = 4
 PEERS = 16
 PAIRS = 4
-PIECES = 4
+PIECES = 2
 PER = KVHEADS // PIECES
 WIDE = PER * 2 * HEAD
 GROUPS = 2
@@ -146,13 +146,13 @@
 
 
 def kernel(
-    image_ref,
-    dest_ref,
-    kimg_ref,
-    seen_ref,
-    gain_ref,
-    qg_ref,
-    kg_ref,
+    image_hbm,
+    dest_hbm,
+    kimg_hbm,
+    seen_hbm,
+    gain_hbm,
+    qg_hbm,
+    kg_hbm,
     x_hbm,
     qkv_hbm,
     out_hbm,
@@ -162,6 +162,13 @@
     att_hbm,
     back_hbm,
     tab_hbm,
+    image_ref,
+    dest_ref,
+    kimg_ref,
+    seen_ref,
+    gain_ref,
+    qg_ref,
+    kg_ref,
     x_ref,
     own_out,
     own_qkv,
@@ -258,11 +265,20 @@
                 (og_hbm, og_ref),
                 (tab_tile, tab_ref),
                 (tab_tile, tab_hbm),
+                (dest_hbm, dest_ref),
+                (seen_hbm, seen_ref),
+                (gain_hbm, gain_ref),
+                (image_hbm, image_ref),
+                (kimg_hbm, kimg_ref),
+                (qg_hbm, qg_ref),
+                (kg_hbm, kg_ref),
             )
         )
     ]
-    qkv_copy, x_copy, out_copy, kv_copy, q_copy, og_copy, tab_copy, tab_out = copies
-    for copy in copies[:-2]:
+    qkv_copy, x_copy, out_copy, kv_copy, q_copy, og_copy, tab_copy, tab_out = copies[:8]
+    dest_copy, seen_copy, gain_copy = copies[8:11]
+    late = copies[11:]
+    for copy in [qkv_copy] + copies[8:] + copies[1:6]:
         copy.start()
 
     barrier = pltpu.get_barrier_semaphore()
@@ -280,6 +296,8 @@
     sub = lax.broadcasted_iota(jnp.int32, (8, 128), 0)
     lane = lax.broadcasted_iota(jnp.int32, (8, 128), 1)
     tile = jnp.zeros((8, 128), jnp.int32)
+    for copy in (dest_copy, seen_copy, gain_copy):
+        copy.wait()
     for block in range(8):
         tile = jnp.where(sub == block, dest_ref[block], tile)
     dest_tile[...] = tile
@@ -396,6 +414,20 @@
                 yield
         yield
 
+    def query_jobs():
+        q_copy.wait()
+        for copy in late:
+            copy.wait()
+        for g in range(KVHEADS):
+            block = q_ref[:, g * SHARED * HEAD : (g + 1) * SHARED * HEAD]
+            for hh in range(SHARED):
+                x = block[:, hh * HEAD : (hh + 1) * HEAD].astype(f32)
+                inv = lax.rsqrt(jnp.mean(x * x, axis=-1, keepdims=True) + EPS)
+                y = (x * inv * qg_ref[...]).astype(bf16)
+                for s in range(CAP):
+                    qn[g, s, hh * LEN : (hh + 1) * LEN, :] = y[s * LEN : (s + 1) * LEN, :]
+            yield
+
     def out_jobs(k):
         if k < 0:
             plane = e
@@ -412,7 +444,7 @@
         out_ref[rows, :] = jnp.concatenate(both, axis=0).astype(bf16)
         yield
 
-    queue = [norm_jobs(), table_jobs(), plane_jobs(-1)]
+    queue = [norm_jobs(), table_jobs(), plane_jobs(-1), query_jobs()]
 
     def pump(steps):
         while queue and steps > 0:
@@ -560,19 +592,6 @@
                 )
             exchange(pay[a][b], got1[a][b], q, f_send.at[0, a, b], f_recv.at[0, a, b])
 
-    q_copy.wait()
-
-    def norm_queries(g, carry):
-        block = q_ref[:, pl.ds(pl.multiple_of(g * SHARED * HEAD, HEAD), SHARED * HEAD)]
-        for hh in range(SHARED):
-            x = block[:, hh * HEAD : (hh + 1) * HEAD].astype(f32)
-            inv = lax.rsqrt(jnp.mean(x * x, axis=-1, keepdims=True) + EPS)
-            y = (x * inv * qg_ref[...]).astype(bf16)
-            for s in range(CAP):
-                qn[g, s, hh * LEN : (hh + 1) * LEN, :] = y[s * LEN : (s + 1) * LEN, :]
-        return carry
-
-    lax.fori_loop(0, KVHEADS, norm_queries, 0)
     og_copy.wait()
 
     def shuffle(got, out, table):
@@ -597,6 +616,7 @@
         at = pl.multiple_of(gi * 2 * HEAD, 2 * HEAD)
         group = h * PER // GROUP
         from_col = pl.multiple_of((h * PER % GROUP + gi) * 2 * HEAD, 2 * HEAD)
+        yield
         blocks, masks = [], []
         seen = seen_rows[pl.ds(s, 1), :]
         for kb in range(CAP):
@@ -613,6 +633,7 @@
         values = keyval[:, HEAD:]
         inv = lax.rsqrt(jnp.mean(keys * keys, axis=-1, keepdims=True) + EPS)
         kn = (keys * inv * kg_ref[...]).astype(bf16)
+        yield
         queries = qn[g, s]
         rows = pl.ds(pl.multiple_of(s * LEN, LEN), LEN)
         cols = pl.ds(pl.multiple_of(g * SHARED * HEAD, SHARED * HEAD), SHARED * HEAD)
@@ -621,17 +642,23 @@
             [grad_row[:, hh * HEAD : (hh + 1) * HEAD] for hh in range(SHARED)], axis=0
         )
         scale = 1.0 / math.sqrt(HEAD)
-        weights = softmax_over_rows(dot_nt(kn, queries), allowed, scale)
+        scores = dot_nt(kn, queries)
+        grad_dot = dot_nt(values, grads)
+        yield
+        weights = softmax_over_rows(scores, allowed, scale)
         rounded = weights.astype(bf16)
+        yield
         attended = dot_tn(rounded, values).astype(bf16)
         att_ref[rows, cols] = jnp.concatenate(
             [attended[hh * LEN : (hh + 1) * LEN, :] for hh in range(SHARED)], axis=1
         )
         grad_values = dot_nn(rounded, grads)
-        grad_dot = dot_nt(values, grads)
+        yield
         delta = jnp.sum(weights * grad_dot, axis=0, keepdims=True)
         grad_scores = (weights * (grad_dot - delta) * scale).astype(bf16)
+        yield
         gained = dot_nn(grad_scores, queries) * kg_ref[...]
+        yield
         mean = jnp.mean(keys * gained, axis=-1, keepdims=True)
         grad_keys = inv * (gained - keys * inv * inv * mean)
         result = jnp.concatenate([grad_keys, grad_values], axis=1).astype(bf16)
@@ -644,8 +671,9 @@
 
         def body(step, carry):
             gi, s = step // (CAP // 2), lax.rem(step, CAP // 2) * 2
-            one(h, gi, s)
-            one(h, gi, s + 1)
+            both = [one(h, gi, s), one(h, gi, s + 1)]
+            while both:
+                both = [steps for steps in both if next(steps, both) is not both]
             return carry
 
         lax.fori_loop(0, PER * CAP // 2, body, 0)
@@ -699,7 +727,7 @@
         done(weight.at[side(m), e], m_send.at[k])
 
 
-def place_kernel(tab_ref, att_hbm, back_hbm, att_out, kvg_out, att, back, kvg, sems):
+def place_kernel(tab_hbm, att_hbm, back_hbm, att_out, kvg_out, tab_ref, att, back, kvg, sems):
     parts = 4
     rows = att.shape[0] // parts
     att_in, back_in, att_back, kvg_back = [], [], [], []
@@ -712,9 +740,10 @@
     for j in range(PAIRS):
         view = pl.ds(2 * j, 2)
         kvg_back.append(pltpu.make_async_copy(kvg.at[view], kvg_out.at[view], sems.at[3, j]))
-    for copy in back_in + att_in:
+    tab_in = pltpu.make_async_copy(tab_hbm, tab_ref, sems.at[4, 0])
+    for copy in [tab_in] + back_in + att_in:
         copy.start()
-    for copy in back_in:
+    for copy in [tab_in] + back_in:
         copy.wait()
     half = KVHEADS * HEAD
     for j in range(PAIRS):
@@ -733,8 +762,6 @@
         copy.wait()
 
 
-VMEM = pl.BlockSpec(memory_space=pltpu.VMEM)
-SMEM = pl.BlockSpec(memory_space=pltpu.SMEM)
 HBM = pl.BlockSpec(memory_space=pltpu.HBM)
 LIMIT = 62 * 1024 * 1024
 
@@ -766,9 +793,16 @@
             jax.ShapeDtypeStruct((PIECES, PEERS, BLK // 2, WIDE), bf16),
             jax.ShapeDtypeStruct((8, 128), jnp.int32),
         ),
-        in_specs=[SMEM] * 3 + [VMEM] * 4 + [HBM] * 6,
+        in_specs=[HBM] * 13,
         out_specs=(HBM, HBM, HBM),
         scratch_shapes=[
+            pltpu.SMEM(block_image.shape, jnp.int32),
+            pltpu.SMEM(block_dest.shape, jnp.int32),
+            pltpu.SMEM(key_image.shape, jnp.int32),
+            pltpu.VMEM((1, CAP * LEN), jnp.int32),
+            pltpu.VMEM((vis // 128, 128), f32),
+            pltpu.VMEM((1, HEAD), f32),
+            pltpu.VMEM((1, HEAD), f32),
             pltpu.VMEM((PAIRS, 2 * BLK, vis), bf16),
             pltpu.VMEM(vit_out.shape, bf16),
             pltpu.VMEM(vit_qkv.shape, bf16),
@@ -798,7 +832,7 @@
             buffers,
             buffers,
             buffers,
-            dma((8,)),
+            dma((15,)),
             dma((2,)),
             dma((2, 2)),
             dma((2,)),
@@ -836,13 +870,14 @@
             jax.ShapeDtypeStruct(queries.shape, bf16),
             jax.ShapeDtypeStruct((enc_blocks, block_len, 2 * KVHEADS * HEAD), bf16),
         ),
-        in_specs=[SMEM, HBM, HBM],
+        in_specs=[HBM, HBM, HBM],
         out_specs=(HBM, HBM),
         scratch_shapes=[
+            pltpu.SMEM((8, 128), jnp.int32),
             pltpu.VMEM(queries.shape, bf16),
             pltpu.VMEM((PIECES, PEERS, BLK // 2, WIDE), bf16),
             pltpu.VMEM((enc_blocks, block_len, 2 * KVHEADS * HEAD), bf16),
-            dma((4, 4)),
+            dma((5, 4)),
         ],
         compiler_params=pltpu.CompilerParams(vmem_limit_bytes=LIMIT),
     )(tables, attended, back)

time: 99.5 us -> 95.4 us (0.959)
  Pallas kernels: 98 us -> 93.9 us
    pallas_call x1, Pallas kernels: 94.6 us -> 91.2 us  [local(): pl.pallas_call(kernel, out_shape=(jax.ShapeDtypeStruct(queries.shape, bf1...]
where the time goes in v4:
time: 95.4 us; the launch traced here: 94.5 us
  Pallas kernels  93.9 us (98%)
    pallas_call x1, Pallas kernels, local(): pl.pallas_call(kernel, out_shape=(jax.ShapeDtypeStruct(queries.shape, bf1...  91.2 us
    pallas_call x1, Pallas kernels, local(): pl.pallas_call(place_kernel, out_shape=(jax.ShapeDtypeStruct(queries.shap...  2.73 us

profile of v4, /device:TPU:32, one launch (start us, length us, event | category | flops | bytes accessed | tf_op | source)
XLA Modules:
  0.0 94.5 jit_solution(2227925751895345820)
XLA Ops:
  0.6 91.2 %shard_map.140 = (bf16[128,4096]{1,0:T(8,128)(2,1)}, bf16[2,16,32,512]{3,2,1,0:T(8,128)(2,1)}, s32[8,128]{1,0:T(8,128)}) custom-call(s32[8]{0:T(128)} %image_hbm.1, s32[8]{0:T(128)} %dest_hbm.1, s32[4,4]{1,0:T(4,128)} %kimg_hbm.1, s32[1,128]{1,0:T(1,128)} %bitcast.7, f32[10,128]{1,0:T(8,128)} %bitcast.6, f32[1,128]{1,0:T(1,128)} %bitcast.8, ...), custom_call_target="tpu_custom_call" | custom-call | tf_op jit(solution)/shard_map/pallas_call | solution.py:789
  91.8 2.7 %shard_map.141 = (bf16[128,4096]{1,0:T(8,128)(2,1)}, bf16[8,64,1024]{2,1,0:T(8,128)(2,1)}) custom-call(s32[8,128]{1,0:T(8,128)} %get-tuple-element.5.tab_hbm, bf16[128,4096]{1,0:T(8,128)(2,1)} %get-tuple-element.6.att_hbm, bf16[2,16,32,512]{3,2,1,0:T(8,128)(2,1)} %get-tuple-element.7.back_hbm), custom_call_target="tpu_custom_call" | custom-call | tf_op jit(solution)/shard_map/pallas_call | solution.py:867

commit v5 on v4

--- a/solution.py
+++ b/solution.py
@@ -669,14 +669,13 @@
             for a in range(2):
                 wait_all(got2[h * PER // GROUP], f_recv.at[1, a, h * PER // GROUP])
 
-        def body(step, carry):
-            gi, s = step // (CAP // 2), lax.rem(step, CAP // 2) * 2
-            both = [one(h, gi, s), one(h, gi, s + 1)]
-            while both:
-                both = [steps for steps in both if next(steps, both) is not both]
+        def body(gi, carry):
+            running = [one(h, gi, s) for s in range(CAP)]
+            while running:
+                running = [steps for steps in running if next(steps, running) is not running]
             return carry
 
-        lax.fori_loop(0, PER * CAP // 2, body, 0)
+        lax.fori_loop(0, PER, body, 0)
 
         def pack(cb, carry):
             block = gkv[tab_ref[5, cb] & 15]

time: 95.4 us -> 93.6 us (0.981)
  Pallas kernels: 93.9 us -> 92.1 us
    pallas_call x1, Pallas kernels: 91.2 us -> 89.3 us  [local(): pl.pallas_call(kernel, out_shape=(jax.ShapeDtypeStruct(queries.shape, bf1...]
where the time goes in v5:
time: 93.6 us; the launch traced here: 92.9 us
  Pallas kernels  92.1 us (98%)
    pallas_call x1, Pallas kernels, local(): pl.pallas_call(kernel, out_shape=(jax.ShapeDtypeStruct(queries.shape, bf1...  89.3 us
    pallas_call x1, Pallas kernels, local(): pl.pallas_call(place_kernel, out_shape=(jax.ShapeDtypeStruct(queries.shap...  2.73 us

profile of v5, /device:TPU:32, one launch (start us, length us, event | category | flops | bytes accessed | tf_op | source)
XLA Modules:
  0.0 92.9 jit_solution(13585390756649432683)
XLA Ops:
  0.6 89.3 %shard_map.140 = (bf16[128,4096]{1,0:T(8,128)(2,1)}, bf16[2,16,32,512]{3,2,1,0:T(8,128)(2,1)}, s32[8,128]{1,0:T(8,128)}) custom-call(s32[8]{0:T(128)} %image_hbm.1, s32[8]{0:T(128)} %dest_hbm.1, s32[4,4]{1,0:T(4,128)} %kimg_hbm.1, s32[1,128]{1,0:T(1,128)} %bitcast.7, f32[10,128]{1,0:T(8,128)} %bitcast.6, f32[1,128]{1,0:T(1,128)} %bitcast.8, ...), custom_call_target="tpu_custom_call" | custom-call | tf_op jit(solution)/shard_map/pallas_call | solution.py:788
  90.0 2.7 %shard_map.141 = (bf16[128,4096]{1,0:T(8,128)(2,1)}, bf16[8,64,1024]{2,1,0:T(8,128)(2,1)}) custom-call(s32[8,128]{1,0:T(8,128)} %get-tuple-element.5.tab_hbm, bf16[128,4096]{1,0:T(8,128)(2,1)} %get-tuple-element.6.att_hbm, bf16[2,16,32,512]{3,2,1,0:T(8,128)(2,1)} %get-tuple-element.7.back_hbm), custom_call_target="tpu_custom_call" | custom-call | tf_op jit(solution)/shard_map/pallas_call | solution.py:866

commit v6 on v5

--- a/solution.py
+++ b/solution.py
@@ -687,8 +687,8 @@
         cols = slice(h * PER * SHARED * HEAD, (h + 1) * PER * SHARED * HEAD)
         pltpu.make_async_copy(att_ref.at[:, cols], att_hbm.at[:, cols], att_sem.at[h]).start()
 
-    for a in range(2):
-        for b in range(GROUPS):
+    for b in range(GROUPS):
+        for a in range(2):
             relay(a, b)
     for h in range(PIECES):
         attend(h)

time: 93.6 us -> 93.1 us (level)
  no operation moved by 1% of the time
where the time goes in v6:
time: 93.1 us; the launch traced here: 92.8 us
  Pallas kernels  92 us (99%)
    pallas_call x1, Pallas kernels, local(): pl.pallas_call(kernel, out_shape=(jax.ShapeDtypeStruct(queries.shape, bf1...  89.3 us
    pallas_call x1, Pallas kernels, local(): pl.pallas_call(place_kernel, out_shape=(jax.ShapeDtypeStruct(queries.shap...  2.73 us

profile of v6, /device:TPU:32, one launch (start us, length us, event | category | flops | bytes accessed | tf_op | source)
XLA Modules:
  0.0 92.8 jit_solution(13924443592826324744)
XLA Ops:
  0.6 89.3 %shard_map.140 = (bf16[128,4096]{1,0:T(8,128)(2,1)}, bf16[2,16,32,512]{3,2,1,0:T(8,128)(2,1)}, s32[8,128]{1,0:T(8,128)}) custom-call(s32[8]{0:T(128)} %image_hbm.1, s32[8]{0:T(128)} %dest_hbm.1, s32[4,4]{1,0:T(4,128)} %kimg_hbm.1, s32[1,128]{1,0:T(1,128)} %bitcast.7, f32[10,128]{1,0:T(8,128)} %bitcast.6, f32[1,128]{1,0:T(1,128)} %bitcast.8, ...), custom_call_target="tpu_custom_call" | custom-call | tf_op jit(solution)/shard_map/pallas_call | solution.py:788
  89.9 2.7 %shard_map.141 = (bf16[128,4096]{1,0:T(8,128)(2,1)}, bf16[8,64,1024]{2,1,0:T(8,128)(2,1)}) custom-call(s32[8,128]{1,0:T(8,128)} %get-tuple-element.5.tab_hbm, bf16[128,4096]{1,0:T(8,128)(2,1)} %get-tuple-element.6.att_hbm, bf16[2,16,32,512]{3,2,1,0:T(8,128)(2,1)} %get-tuple-element.7.back_hbm), custom_call_target="tpu_custom_call" | custom-call | tf_op jit(solution)/shard_map/pallas_call | solution.py:866
